TPU v7x, 128 devices: a whole 4x4x4 slice. The times are simulated.
128 devices in a mesh: tm: 32 (over y, x, z_hi), row: 2 (over z_lo), col: 2 (over core).
Axes of the slice: x: 4, y: 4, z: 4 (z_hi: 2, z_lo: 2; z = z_hi * 2 + z_lo), core: 2. Of those that a mesh axis runs over, the one named last changes fastest.
Arguments:
- strain: float32 [24576, 2048], P('tm', ('row', 'col')), may hold values from -6 to 6
Outputs:
- lag_corr: float32 [2048, 8, 2048], P(('tm', 'row'), None, 'col')
All inputs are finite; a program needn't handle non-finite values.
Results may differ from a plain program's by a relative error of at most 0.0001.
Values sent between devices are 32-bit elements; how exact they have to be, the bound alone decides.
A program may use at most 192 MiB of HBM per device.

v0:
```python
import jax
import jax.numpy as jnp
from jax import lax
from jax.sharding import PartitionSpec as P

LAGS = 8


def passed_along(block, axis, distance):
    devices = range(lax.axis_size(axis))
    route = [(i - distance, i) for i in devices if i - distance in devices]
    return lax.ppermute(block, axis, route)


def shards(strain):
    length = strain.shape[0]
    whole = lax.all_gather(strain, ("row", "col"), axis=1, tiled=True)
    ahead = passed_along(whole[:LAGS], "tm", -1)
    extended = jnp.concatenate([whole, ahead], axis=0)
    tm_count = lax.axis_size("tm")
    row_count = lax.axis_size("row")
    col_count = lax.axis_size("col")
    channels = whole.shape[1]
    band = channels // (tm_count * row_count)
    width = channels // col_count
    samples = length * tm_count
    row_index = lax.axis_index("row")
    col_index = lax.axis_index("col")
    shaped = extended.reshape(length + LAGS, tm_count, row_count, band)
    row_panel = lax.dynamic_index_in_dim(shaped, row_index, 2, keepdims=False).reshape(
        length + LAGS, tm_count * band
    )
    col_panel = lax.dynamic_slice_in_dim(whole, col_index * width, width, 1)
    pieces = []
    for lag in range(1, LAGS + 1):
        lagged = row_panel[lag : lag + length]
        prod = jnp.einsum(
            "ti,tj->ij",
            lagged,
            col_panel,
            precision=lax.Precision.HIGHEST,
            preferred_element_type=jnp.float32,
        )
        pieces.append(prod / jnp.sqrt(jnp.float32(samples - lag)))
    terms = jnp.stack(pieces, axis=1)
    return lax.psum_scatter(terms, "tm", scatter_dimension=0, tiled=True)


def solution(mesh):
    placed = (P("tm", ("row", "col")),)
    return jax.shard_map(
        shards, mesh=mesh, in_specs=placed, out_specs=P(("tm", "row"), None, "col"), check_vma=False
    )
```

profile of v0, /device:TPU:1, one launch (start us, length us, event | category | flops | bytes accessed | tf_op | source)
XLA Modules:
  0.0 933.0 jit_solution(13607343563796796121)
XLA Ops:
  6.5 0.0 all-gather.2.cloned.1.call-start
  6.5 3.0 copy.5
  9.6 0.0 all-gather.2.cloned.1.call-update
  9.6 0.0 reduce-scatter.2.cloned.1.call-start
  9.7 67.8 %all-gather.2.cloned.1.call-done = f32[768,2048]{0,1:T(8,128)} async-done(((f32[768,512]{0,1:T(8,128)}), f32[768,2048]{0,1:T(8,128)}) %all-gather.2.cloned.1.call-update) | async-done | bytes 6291472 | tf_op jit(solution)/shard_map/all_gather | solution.py:17
  77.4 1.3 slice.68
  78.7 0.3 copy.6
  79.0 1.3 collective-permute-start
  80.3 5.8 collective-permute-done
  86.2 0.3 copy.7
  86.5 6.2 pad_maximum_fusion
  92.7 19.1 %constant_dynamic-slice_fusion.7 = (f32[768,32,1,32]{0,3,2,1:T(8,128)S(1)}, f32[768,32,1,32]{0,3,2,1:T(8,128)}, f32[768,32,1,32]{0,3,2,1:T(8,128)}, f32[768,32,1...) fusion(f32[776,32,2,32]{0,3,2,1:T(8,128)} %bitcast.33, ...), kind=kLoop, calls=%fused_computation.32 | loop fusion | bytes 50331684 | tf_op jit(solution)/shard_map/slice | solution.py:36
  111.9 0.0 copy-start.5
  111.9 0.0 slice-start
  111.9 14.1 %bitcast_dynamic-update-slice_fusion.7 = f32[1024,8,1024]{2,0,1:T(8,128)} fusion(f32[768,1024]{0,1:T(8,128)} %bitcast.43, f32[768,2048]{0,1:T(8,128)} %all-gather.2.cloned.1.call-done, s32[]{:T(128)S(6)} %select_n.8), kind=kOutput, calls=%fused_computation.8 | convolution fusion | flops 9664724992 | bytes 10485764 | tf_op jit(solution)/shard_map/ti,tj->ij/dot_general | solution.py:37
  126.0 0.0 copy-done.5
  126.0 0.0 slice-start.1
  126.0 0.0 copy-start.4
  126.0 13.3 %bitcast_dynamic-update-slice_fusion.6 = f32[1024,8,1024]{2,0,1:T(8,128)} fusion(f32[1024,8,1024]{2,0,1:T(8,128)} %bitcast_dynamic-update-slice_fusion.7, f32[768,1024]{0,1:T(8,128)S(1)} %bitcast.42, f32[768,2048]{0,1:T(8,128)} %all-gather.2.cloned.1.call-done, s32[]{:T(128)S(6)} %select_n.8), kind=kOutput, calls=%fused_computation.7 | convolution fusion | flops 9664724992 | bytes 10485764 | tf_op jit(solution)/shard_map/ti,tj->ij/dot_general | solution.py:37
  139.3 0.0 slice-done
  139.3 0.0 slice-done.1
  139.3 0.0 copy-done.4
  139.3 0.0 copy-start.3
  139.3 11.6 %bitcast_dynamic-update-slice_fusion.5 = f32[1024,8,1024]{2,0,1:T(8,128)} fusion(f32[1024,8,1024]{2,0,1:T(8,128)} %bitcast_dynamic-update-slice_fusion.6, f32[768,1024]{0,1:T(8,128)S(1)} %bitcast.41, f32[768,2048]{0,1:T(8,128)S(1)} %bitcast.35, s32[]{:T(128)S(6)} %select_n.8), kind=kOutput, calls=%fused_computation.6 | convolution fusion | flops 9664724992 | bytes 10485764 | tf_op jit(solution)/shard_map/ti,tj->ij/dot_general | solution.py:37
  150.9 0.0 copy-done.3
  150.9 0.0 copy-start.2
  150.9 11.7 %bitcast_dynamic-update-slice_fusion.4 = f32[1024,8,1024]{2,0,1:T(8,128)} fusion(f32[1024,8,1024]{2,0,1:T(8,128)} %bitcast_dynamic-update-slice_fusion.5, f32[768,1024]{0,1:T(8,128)S(1)} %bitcast.40, f32[768,2048]{0,1:T(8,128)S(1)} %bitcast.35, s32[]{:T(128)S(6)} %select_n.8), kind=kOutput, calls=%fused_computation.5 | convolution fusion | flops 9664724992 | bytes 10485764 | tf_op jit(solution)/shard_map/ti,tj->ij/dot_general | solution.py:37
  162.6 0.0 copy-done.2
  162.6 0.0 copy-start.1
  162.6 11.5 %bitcast_dynamic-update-slice_fusion.3 = f32[1024,8,1024]{2,0,1:T(8,128)} fusion(f32[1024,8,1024]{2,0,1:T(8,128)} %bitcast_dynamic-update-slice_fusion.4, f32[768,1024]{0,1:T(8,128)S(1)} %bitcast.39, f32[768,2048]{0,1:T(8,128)S(1)} %bitcast.35, s32[]{:T(128)S(6)} %select_n.8), kind=kOutput, calls=%fused_computation.4 | convolution fusion | flops 9664724992 | bytes 10485764 | tf_op jit(solution)/shard_map/ti,tj->ij/dot_general | solution.py:37
  174.2 0.0 copy-done.1
  174.2 0.0 copy-start
  174.2 12.0 %bitcast_dynamic-update-slice_fusion.2 = f32[1024,8,1024]{2,0,1:T(8,128)} fusion(f32[1024,8,1024]{2,0,1:T(8,128)} %bitcast_dynamic-update-slice_fusion.3, f32[768,1024]{0,1:T(8,128)S(1)} %bitcast.38, f32[768,2048]{0,1:T(8,128)S(1)} %bitcast.35, s32[]{:T(128)S(6)} %select_n.8), kind=kOutput, calls=%fused_computation.3 | convolution fusion | flops 9664724992 | bytes 10485764 | tf_op jit(solution)/shard_map/ti,tj->ij/dot_general | solution.py:37
  186.1 0.0 copy-done
  186.1 11.5 %bitcast_dynamic-update-slice_fusion.1 = f32[1024,8,1024]{2,0,1:T(8,128)} fusion(f32[1024,8,1024]{2,0,1:T(8,128)} %bitcast_dynamic-update-slice_fusion.2, f32[768,1024]{0,1:T(8,128)S(1)} %bitcast.37, f32[768,2048]{0,1:T(8,128)S(1)} %bitcast.35, s32[]{:T(128)S(6)} %select_n.8), kind=kOutput, calls=%fused_computation.2 | convolution fusion | flops 9664724992 | bytes 10485764 | tf_op jit(solution)/shard_map/ti,tj->ij/dot_general | solution.py:37
  197.7 11.7 %bitcast_dynamic-update-slice_fusion = f32[1024,8,1024]{2,0,1:T(8,128)} fusion(f32[1024,8,1024]{2,0,1:T(8,128)} %bitcast_dynamic-update-slice_fusion.1, f32[768,1024]{0,1:T(8,128)S(1)} %bitcast.36, f32[768,2048]{0,1:T(8,128)S(1)} %bitcast.35, s32[]{:T(128)S(6)} %select_n.8), kind=kOutput, calls=%fused_computation.1 | convolution fusion | flops 9664724992 | bytes 10485764 | tf_op jit(solution)/shard_map/ti,tj->ij/dot_general | solution.py:37
  209.4 0.0 reduce-scatter.2.cloned.1.call-update
  209.5 713.7 %reduce-scatter.2.cloned.1.call-done = f32[32,8,1024]{2,0,1:T(8,128)} async-done(((f32[1024,8,1024]{2,0,1:T(8,128)}), f32[32,8,1024]{2,0,1:T(8,128)}) %reduce-scatter.2.cloned.1.call-update) | async-done | bytes 1048592 | tf_op jit(solution)/shard_map/reduce_scatter | solution.py:46
  923.2 2.8 copy.8
  (1 shorter events, 0.0 us)
Async XLA Ops:
  6.5 70.9 %all-gather.2.cloned.1.call-start = ((), (), s32[]{:S(2)}) async-start(), calls=%async_computation.1 | async-start | bytes 7864320 | tf_op jit(solution)/shard_map/all_gather | solution.py:17
  9.6 913.6 %reduce-scatter.2.cloned.1.call-start = ((), (), s32[]{:S(2)}) async-start(), calls=%async_computation.2 | async-start | bytes 34603008 | tf_op jit(solution)/shard_map/reduce_scatter | solution.py:46
  79.0 7.2 collective-permute-start
  111.9 14.1 %copy-start.5 = (f32[768,32,1,32]{0,3,2,1:T(8,128)S(1)}, f32[768,32,1,32]{0,3,2,1:T(8,128)}, u32[]{:S(2)}) copy-start(f32[768,32,1,32]{0,3,2,1:T(8,128)} %get-tuple-element.11) | copy-start | bytes 9437188
  111.9 27.4 %slice-start = ((s8[6291456]{0:T(1024)(128)(4,1)}), s8[4194304]{0:T(1024)(128)(4,1)S(1)}, s32[]{:S(2)}) async-start(s8[6291456]{0:T(1024)(128)(4,1)} %bitcast.34), calls=%async_computation.3 | async-start | bytes 8388608
  126.0 13.3 %slice-start.1 = ((s8[6291456]{0:T(1024)(128)(4,1)}), s8[2097152]{0:T(1024)(128)(4,1)S(1)}, s32[]{:S(2)}) async-start(s8[6291456]{0:T(1024)(128)(4,1)} %bitcast.34), calls=%async_computation.4 | async-start | bytes 4194304
  126.0 13.3 %copy-start.4 = (f32[768,32,1,32]{0,3,2,1:T(8,128)S(1)}, f32[768,32,1,32]{0,3,2,1:T(8,128)}, u32[]{:S(2)}) copy-start(f32[768,32,1,32]{0,3,2,1:T(8,128)} %get-tuple-element.10) | copy-start | bytes 9437188
  139.3 11.6 %copy-start.3 = (f32[768,32,1,32]{0,3,2,1:T(8,128)S(1)}, f32[768,32,1,32]{0,3,2,1:T(8,128)}, u32[]{:S(2)}) copy-start(f32[768,32,1,32]{0,3,2,1:T(8,128)} %get-tuple-element.9) | copy-start | bytes 9437188
  150.9 11.7 %copy-start.2 = (f32[768,32,1,32]{0,3,2,1:T(8,128)S(1)}, f32[768,32,1,32]{0,3,2,1:T(8,128)}, u32[]{:S(2)}) copy-start(f32[768,32,1,32]{0,3,2,1:T(8,128)} %get-tuple-element.8) | copy-start | bytes 9437188
  162.6 11.6 %copy-start.1 = (f32[768,32,1,32]{0,3,2,1:T(8,128)S(1)}, f32[768,32,1,32]{0,3,2,1:T(8,128)}, u32[]{:S(2)}) copy-start(f32[768,32,1,32]{0,3,2,1:T(8,128)} %get-tuple-element.7) | copy-start | bytes 9437188
  174.2 12.0 %copy-start = (f32[768,32,1,32]{0,3,2,1:T(8,128)S(1)}, f32[768,32,1,32]{0,3,2,1:T(8,128)}, u32[]{:S(2)}) copy-start(f32[768,32,1,32]{0,3,2,1:T(8,128)} %get-tuple-element.6) | copy-start | bytes 9437188
Sparse Core Ops, SparseCore 0:
  9.7 67.6 all-gather.1
  209.6 713.5 reduce-scatter.1
where the time goes:
time: 941 us; the launch traced here: 933 us
  waiting for transfers between devices  787 us (84%)
  matrix products  97.5 us (10%)
  local copies, waits for them, and re-layouts  26.9 us (3%)
  between operations  13.7 us (1%)
    reduce_scatter x1, waiting for transfers between devices, shards(): return lax.psum_scatter(terms, 'tm', scatter_dimension=0, tiled=True)  714 us
    dot_general x8, matrix products, shards(): jnp.einsum('ti,tj->ij', lagged, col_panel, precision=lax.Precision.HIGHES...  97.5 us
    all_gather x1, waiting for transfers between devices, shards(): whole = lax.all_gather(strain, ('row', 'col'), axis=1, tiled=True)  67.8 us
    slice x1, local copies, waits for them, and re-layouts, shards(): lagged = row_panel[lag:lag + length]  19.1 us
  transfers between devices with their start and end apart: 3, of which 3 were waited for; matrix products, arithmetic and copies ran while one was open for 0% of the time, Pallas kernels for 0%

commit v1 on v0

v1 whole, which is shorter than its diff:
```python
import functools

import jax
import jax.numpy as jnp
import numpy as np
from jax import lax
from jax.experimental import pallas as pl
from jax.experimental.pallas import tpu as pltpu
from jax.sharding import PartitionSpec as P

MESH = pl.DeviceIdType.MESH
LAGS = 8
SAMPLES = 24576
LEN = 768
LANES = 128
PER = LEN // LAGS
DEEP = 4 * PER
WIDE = 2 * LANES
F32 = jnp.float32
BF16 = jnp.bfloat16


def halves(v):
    hi = v.astype(BF16)
    return hi, (v - hi.astype(F32)).astype(BF16)


def kernel(
    s_ref, out_ref, blocks, firsts, halo, halo_out, x_hi, x_lo, y_hi, y_lo, part, far_in, near_in, last_in,
    load_sem, copy_sem, halo_sem, fan_send, fan_recv, fan_copy, ring_send, ring_recv, z_send, z_recv,
    core_send, core_recv, far_send, far_recv, near_send, near_recv, last_send, last_recv, last_copy,
):
    tm, zl, c = lax.axis_index("tm"), lax.axis_index("row"), lax.axis_index("col")
    y, x, zh = lax.div(tm, 8), lax.rem(lax.div(tm, 2), 4), lax.rem(tm, 2)
    b = zl * 2 + c

    def at(yy, xx, zz, row, col):
        return (lax.rem(yy, 4) * 8 + lax.rem(xx, 4) * 2 + zz, row, col)

    def along_x(d):
        return at(y, x + d, zh, zl, c)

    def along_y(d):
        return at(y + d, x, zh, zl, c)

    before = (lax.rem(tm + 31, 32), zl, c)
    after = (lax.rem(tm + 1, 32), zl, c)
    other_z = (tm, 1 - zl, c)
    other_core = (tm, zl, 1 - c)

    barrier = pltpu.get_barrier_semaphore()
    peers = [along_x(1), along_x(2), along_x(3), along_y(1), along_y(3), before, after]
    peers += [(tm, 1 - zl, c), (tm, 1 - zl, 1 - c), (tm, zl, 1 - c)]
    peers += [at(y, x, 1 - zh, row, col) for row in (0, 1) for col in (0, 1)]
    for peer in peers:
        pl.semaphore_signal(barrier, inc=1, device_id=peer, device_id_type=MESH)

    loads = []
    for q in range(4):
        lanes = pl.ds(pl.multiple_of(lax.rem(x + q, 4) * LANES, LANES), LANES)
        loads.append(pltpu.make_async_copy(s_ref.at[:, lanes], blocks.at[0, q], load_sem.at[q]))
        loads[-1].start()
    pl.semaphore_wait(barrier, len(peers))

    sent = []

    def send(src, dst, send_sem, recv_sem, device):
        copy = pltpu.make_async_remote_copy(
            src_ref=src, dst_ref=dst, send_sem=send_sem, recv_sem=recv_sem, device_id=device, device_id_type=MESH
        )
        copy.start()
        sent.append(copy)
        return copy

    def ring(way, n, d, q):
        step = 3 if way == 0 else 1
        return send(
            blocks.at[d, q],
            blocks.at[(d + step) % 4, (q + step) % 4],
            ring_send.at[way, n],
            ring_recv.at[way, n],
            along_x(1 if way == 0 else 3),
        )

    halo_copy = send(s_ref.at[pl.ds(0, LAGS)], halo, halo_sem.at[0], halo_sem.at[1], before)
    for load in loads:
        load.wait()

    r0, l0 = ring(0, 0, 0, 1), ring(1, 0, 0, 3)
    r1, l1 = ring(0, 1, 0, 2), ring(1, 1, 0, 0)

    halo_copy.wait_recv()
    for p in range(4):
        halo_out[p] = jnp.where(tm == 31, jnp.zeros((LAGS, LANES), F32), halo[:, p * LANES : (p + 1) * LANES])
    tail = pl.ds(LEN, LAGS)
    fans = []
    for d in range(1, 4):
        fans.append(
            send(
                halo_out.at[lax.rem(x + d, 4)],
                firsts.at[b, 4 - d, tail],
                fan_send.at[4 - d],
                fan_recv.at[4 - d],
                along_x(d),
            )
        )
    fan0 = pltpu.make_async_copy(halo_out.at[x], firsts.at[b, 0, tail], fan_copy.at[0])
    fan0.start()

    z_copies, core_copies = {}, {}

    def cross(d, arrived):
        if arrived is not None:
            arrived.wait_recv()
        mine = pltpu.make_async_copy(blocks.at[d, 0], firsts.at[b, d, pl.ds(0, LEN)], copy_sem.at[d])
        mine.start()
        if d == 0:
            fan0.wait()
        else:
            fans[3 - d].wait_recv()
        mine.wait()
        z_copies[d] = send(firsts.at[b, d], firsts.at[b, d], z_send.at[d], z_recv.at[d], other_z)
        core_copies[d] = send(firsts.at[b, d], firsts.at[b, d], core_send.at[0, d], core_recv.at[0, d], other_core)

    def pass_on(d):
        z_copies[d].wait_recv()
        b2 = (1 - zl) * 2 + c
        core_copies[4 + d] = send(
            firsts.at[b2, d], firsts.at[b2, d], core_send.at[1, d], core_recv.at[1, d], other_core
        )

    cross(0, None)
    cross(3, r0)
    cross(1, l0)
    r1.wait_recv()
    r2 = ring(0, 2, 3, 1)
    l2 = ring(1, 2, 1, 0)
    cross(2, r2)
    r3, l3 = ring(0, 3, 0, 3), ring(1, 3, 0, 1)
    r4 = ring(0, 4, 0, 0)
    l1.wait_recv()
    l4 = ring(1, 4, 1, 1)
    r5, l5 = ring(0, 5, 3, 0), ring(1, 5, 0, 2)
    for d in (0, 3, 1, 2):
        pass_on(d)
    l2.wait_recv()

    def seconds(chunk):
        for q in range(2):
            lanes = slice(q * LANES, (q + 1) * LANES)
            for d in range(4):
                for r in range(LAGS):
                    hi, lo = halves(blocks[d, 2 * chunk + q, pl.ds(r, PER, stride=LAGS), :])
                    rows = slice(r * DEEP + d * PER, r * DEEP + (d + 1) * PER)
                    y_hi[rows, lanes] = hi
                    y_lo[rows, lanes] = lo

    def spread(bb, carry):
        for m in range(1, 2 * LAGS):
            v = jnp.concatenate([firsts[bb, d, pl.ds(m, PER, stride=LAGS), :] for d in range(4)], axis=0)
            hi, lo = halves(v.T)
            lanes = slice((m - 1) * DEEP, m * DEEP)
            x_hi[bb, :, lanes] = hi
            x_lo[bb, :, lanes] = lo
        return carry

    def products(chunk, e):
        bb = lax.rem(y + e, 4)

        def dots(n):
            lhs_hi = jnp.concatenate(
                [x_hi[bb, :, pl.ds(pl.multiple_of(n * LEN + k * DEEP, LANES), LEN)] for k in range(LAGS)], axis=0
            )
            lhs_lo = jnp.concatenate(
                [x_lo[bb, :, pl.ds(pl.multiple_of(n * LEN + k * DEEP, LANES), LEN)] for k in range(LAGS)], axis=0
            )
            rows = pl.ds(pl.multiple_of(n * LEN, LEN), LEN)
            rhs_hi, rhs_lo = y_hi[rows, :], y_lo[rows, :]
            got = jnp.dot(lhs_hi, rhs_hi, preferred_element_type=F32)
            got += jnp.dot(lhs_lo, rhs_hi, preferred_element_type=F32)
            got += jnp.dot(lhs_hi, rhs_lo, preferred_element_type=F32)
            return got.reshape(LAGS, LANES, WIDE)

        def step(n, carry):
            part[chunk, e] += dots(n)
            return carry

        part[chunk, e] = dots(0)
        lax.fori_loop(1, 4, step, 0)

    half = [pl.ds(0, LAGS // 2), pl.ds(LAGS // 2, LAGS // 2)]
    fars, nears, lasts = {}, {}, {}

    def near(chunk, way, h):
        e = 1 if way == 0 else 3
        nears[chunk, way, h] = send(
            part.at[chunk, e, half[h]],
            near_in.at[chunk, way, half[h]],
            near_send.at[chunk, way, h],
            near_recv.at[chunk, way, h],
            along_y(e),
        )

    def sums(chunk):
        products(chunk, 2)
        for way in range(2):
            fars[chunk, way] = send(
                part.at[chunk, 2, half[way]],
                far_in.at[chunk, way],
                far_send.at[chunk, way],
                far_recv.at[chunk, way],
                along_y(1 if way == 0 else 3),
            )
        products(chunk, 1)
        near(chunk, 0, 1)
        products(chunk, 3)
        near(chunk, 1, 0)
        products(chunk, 0)

    def add_far(chunk):
        for way in range(2):
            e = 1 if way == 0 else 3
            fars[chunk, way].wait_recv()
            part[chunk, e, half[way]] += far_in[chunk, way]
            near(chunk, way, way)

    def finish(chunk):
        for way in range(2):
            for h in range(2):
                nears[chunk, way, h].wait_recv()
        part[chunk, 0] += near_in[chunk, 0] + near_in[chunk, 1]
        for other in range(2):
            for row in range(2):
                src = part.at[chunk, 0, :, pl.ds(pl.multiple_of((lax.rem(zh + other, 2) * 2 + row) * 32, 32), 32)]
                here = jnp.logical_and(row == zl, zl == c) if other == 0 else False
                copy = pltpu.make_async_remote_copy(
                    src_ref=src,
                    dst_ref=last_in.at[chunk, c, zh],
                    send_sem=last_send.at[chunk, other, row],
                    recv_sem=last_recv.at[chunk, c, zh],
                    device_id=at(y, x, lax.rem(zh + other, 2), row, zl),
                    device_id_type=MESH,
                )
                if other == 0:
                    pl.when(jnp.logical_not(here))(copy.start)
                    own = pltpu.make_async_copy(src, last_in.at[chunk, c, zh], last_copy.at[chunk])
                    lasts[chunk, row] = (here, copy, own)
                    pl.when(here)(own.start)
                else:
                    copy.start()
                    sent.append(copy)

    scale = [np.float32(1.0 / np.sqrt(np.float32(SAMPLES - k))) for k in range(1, LAGS + 1)]

    def write(chunk):
        for row in range(2):
            here, copy, own = lasts[chunk, row]
            pl.when(jnp.logical_not(here))(copy.wait_send)
            pl.when(here)(own.wait)
        for cc in range(2):
            for hh in range(2):
                arrives = jnp.logical_not(jnp.logical_and(zl == c, jnp.logical_and(cc == c, hh == zh)))
                copy = pltpu.make_async_remote_copy(
                    src_ref=last_in.at[chunk, cc, hh],
                    dst_ref=last_in.at[chunk, cc, hh],
                    send_sem=last_send.at[chunk, 0, 0],
                    recv_sem=last_recv.at[chunk, cc, hh],
                    device_id=other_z,
                    device_id_type=MESH,
                )
                pl.when(arrives)(copy.wait_recv)
        for cc in range(2):
            for q in range(2):
                p = lax.rem(x + 2 * chunk + q, 4)
                lanes = pl.ds(pl.multiple_of(cc * 4 * LANES + p * LANES, LANES), LANES)
                for k in range(LAGS):
                    piece = slice(q * LANES, (q + 1) * LANES)
                    total = last_in[chunk, cc, 0, k, :, piece] + last_in[chunk, cc, 1, k, :, piece]
                    out_ref[:, k, lanes] = total * scale[k]

    seconds(0)
    for d in range(4):
        core_copies[d].wait_recv()
        core_copies[4 + d].wait_recv()
    lax.fori_loop(0, 4, spread, 0)
    sums(0)
    add_far(0)
    for copy in (r3, l3, r4, l4, r5, l5):
        copy.wait_recv()
    seconds(1)
    sums(1)
    finish(0)
    add_far(1)
    finish(1)
    write(0)
    write(1)
    for copy in sent:
        copy.wait_send()


def shards(strain):
    dma = pltpu.SemaphoreType.DMA
    return pl.pallas_call(
        kernel,
        out_shape=jax.ShapeDtypeStruct((32, LAGS, 8 * LANES), F32),
        in_specs=[pl.BlockSpec(memory_space=pl.ANY)],
        out_specs=pl.BlockSpec(memory_space=pltpu.VMEM),
        scratch_shapes=[
            pltpu.VMEM((4, 4, LEN, LANES), F32),
            pltpu.VMEM((4, 4, LEN + LAGS, LANES), F32),
            pltpu.VMEM((LAGS, 4 * LANES), F32),
            pltpu.VMEM((4, LAGS, LANES), F32),
            pltpu.VMEM((4, LANES, (2 * LAGS - 1) * DEEP), BF16),
            pltpu.VMEM((4, LANES, (2 * LAGS - 1) * DEEP), BF16),
            pltpu.VMEM((LAGS * DEEP, WIDE), BF16),
            pltpu.VMEM((LAGS * DEEP, WIDE), BF16),
            pltpu.VMEM((2, 4, LAGS, LANES, WIDE), F32),
            pltpu.VMEM((2, 2, LAGS // 2, LANES, WIDE), F32),
            pltpu.VMEM((2, 2, LAGS, LANES, WIDE), F32),
            pltpu.VMEM((2, 2, 2, LAGS, 32, WIDE), F32),
            dma((4,)), dma((4,)), dma((2,)), dma((4,)), dma((4,)), dma((1,)), dma((2, 6)), dma((2, 6)),
            dma((4,)), dma((4,)), dma((2, 4)), dma((2, 4)), dma((2, 2)), dma((2, 2)),
            dma((2, 2, 2)), dma((2, 2, 2)), dma((2, 2, 2)), dma((2, 2, 2)), dma((2,)),
        ],
        compiler_params=pltpu.CompilerParams(
            collective_id=0, has_side_effects=True, vmem_limit_bytes=60 * 2**20
        ),
        cost_estimate=pl.CostEstimate(flops=3 * 2 * 8 * 512 * 512 * 3072, bytes_accessed=2**22, transcendentals=0),
    )(strain)


def solution(mesh):
    placed = (P("tm", ("row", "col")),)
    return jax.shard_map(
        shards, mesh=mesh, in_specs=placed, out_specs=P(("tm", "row"), None, "col"), check_vma=False
    )
```

time: 941 us -> 152 us (0.16)
  waiting for transfers between devices: 787 us -> 0 us
  Pallas kernels: 0 us -> 147 us
  matrix products: 97.5 us -> 0 us
  local copies, waits for them, and re-layouts: 26.9 us -> 2.31 us
  between operations: 13.7 us -> 0.01 us
    reduce_scatter x1 -> x0, waiting for transfers between devices: 714 us -> none  [shards(): return lax.psum_scatter(terms, 'tm', scatter_dimension=0, tiled=True)]
    pallas_call x0 -> x1, Pallas kernels: none -> 147 us  [shards(): pl.pallas_call(kernel, out_shape=jax.ShapeDtypeStruct((32, LAGS, 8 * LANE...]
    dot_general x8 -> x0, matrix products: 97.5 us -> none  [shards(): jnp.einsum('ti,tj->ij', lagged, col_panel, precision=lax.Precision.HIGHES...]
    all_gather x1 -> x0, waiting for transfers between devices: 67.8 us -> none  [shards(): whole = lax.all_gather(strain, ('row', 'col'), axis=1, tiled=True)]
    slice x3 -> x0, local copies, waits for them, and re-layouts: 20.7 us -> none  [the longest x1 19.1 us: shards(): lagged = row_panel[lag:lag + length]]
  transfers between devices with their start and end apart: 3 -> 0, of which waited for: 3 -> 0; matrix products, arithmetic and copies ran while one was open for 0% -> 0% of each run, Pallas kernels for 0% -> 0%
where the time goes in v1:
time: 152 us; the launch traced here: 150 us
  Pallas kernels  147 us (97%)
  local copies, waits for them, and re-layouts  2.31 us (2%)
    pallas_call x1, Pallas kernels, shards(): pl.pallas_call(kernel, out_shape=jax.ShapeDtypeStruct((32, LAGS, 8 * LANE...  147 us

profile of v1, /device:TPU:1, one launch (start us, length us, event | category | flops | bytes accessed | tf_op | source)
XLA Modules:
  0.0 149.7 jit_solution(17116998968572673098)
XLA Ops:
  0.0 147.4 %shard_map.17 = f32[32,8,1024]{2,1,0:T(8,128)} custom-call(f32[768,512]{1,0:T(8,128)} %s_ref.1), custom_call_target="tpu_custom_call" | custom-call | flops 38654705664 | bytes 4194304 | tf_op jit(solution)/shard_map/pallas_call | solution.py:303
  147.4 2.3 %copy.3 = f32[32,8,1024]{2,1,0:T(8,128)} copy(f32[32,8,1024]{2,1,0:T(8,128)} %shard_map.17) | data formatting | bytes 2097152

commit v2 on v0

v2 whole, which is shorter than its diff:
```python
import jax
import jax.numpy as jnp
import numpy as np
from jax import lax
from jax.experimental import pallas as pl
from jax.experimental.pallas import tpu as pltpu
from jax.sharding import PartitionSpec as P

MESH = pl.DeviceIdType.MESH
LAGS = 8
SAMPLES = 24576
LEN = 768
LANES = 128
PER = LEN // LAGS
DEEP = 4 * PER
CHUNKS = ((0, 2), (2, 2))
WIDTHS = tuple(n * LANES for _, n in CHUNKS)
F32 = jnp.float32
BF16 = jnp.bfloat16


def halves(v):
    hi = v.astype(BF16)
    return hi, (v - hi.astype(F32)).astype(BF16)


def kernel(
    s_ref, out_ref, blocks, firsts, heads, heads_z, head_y, tails, x_hi, x_lo, y_hi, y_lo, part, far_in, near_in, last_in,
    load_sem, own_sem, fan_send, fan_recv, fan_own, head_send, head_recv, ring_send, ring_recv, z_send, z_recv,
    core_send, core_recv, far_send, far_recv, near_send, near_recv, last_send, last_recv, last_own, ready,
):
    tm, zl, c = lax.axis_index("tm"), lax.axis_index("row"), lax.axis_index("col")
    y, x, zh = lax.div(tm, 8), lax.rem(lax.div(tm, 2), 4), lax.rem(tm, 2)
    b = zl * 2 + c
    b_z, b_core, b_both = (1 - zl) * 2 + c, zl * 2 + 1 - c, (1 - zl) * 2 + 1 - c

    def at(yy, xx, zz, row, col):
        return (lax.rem(yy, 4) * 8 + lax.rem(xx, 4) * 2 + zz, row, col)

    def along_x(d):
        return at(y, x + d, zh, zl, c)

    def along_y(d):
        return at(y + d, x, zh, zl, c)

    other_z = (tm, 1 - zl, c)
    other_core = (tm, zl, 1 - c)
    other_half = at(y, x, 1 - zh, zl, c)

    barrier = pltpu.get_barrier_semaphore()
    peers = [along_x(1), along_x(3), along_x(2), along_y(1), along_y(3), other_z, other_core, other_half]
    for peer in peers:
        pl.semaphore_signal(barrier, inc=1, device_id=peer, device_id_type=MESH)

    loads = []
    for q in (1, 3, 2, 0):
        lanes = pl.ds(pl.multiple_of(lax.rem(x + q, 4) * LANES, LANES), LANES)
        loads.append(pltpu.make_async_copy(s_ref.at[:, lanes], blocks.at[0, q], load_sem.at[q]))
        loads[-1].start()
    for load in loads:
        load.wait()
    pl.semaphore_wait(barrier, len(peers))

    sent = []

    def send(src, dst, send_sem, recv_sem, device):
        copy = pltpu.make_async_remote_copy(
            src_ref=src, dst_ref=dst, send_sem=send_sem, recv_sem=recv_sem, device_id=device, device_id_type=MESH
        )
        copy.start()
        sent.append(copy)
        return copy

    def ring(n, way, d, q):
        return send(
            blocks.at[d, q],
            blocks.at[(d - way) % 4, (q - way) % 4],
            ring_send.at[n],
            ring_recv.at[n],
            along_x(way % 4),
        )

    fans = []
    for d in range(1, 4):
        fans.append(
            send(blocks.at[0, d, pl.ds(0, LAGS)], heads.at[x], fan_send.at[4 - d], fan_recv.at[4 - d], along_x(d))
        )
    fan_mine = pltpu.make_async_copy(blocks.at[0, 0, pl.ds(0, LAGS)], heads.at[x], fan_own.at[0])
    fan_mine.start()

    from_left = ring(0, 1, 0, 1)
    from_right = ring(1, -1, 0, 3)

    z_copies, core_copies, own_copies = {}, {}, {}
    rows = pl.ds(0, LEN)
    tail = pl.ds(LEN, LAGS)
    farthest = lax.rem(y + 2, 4)

    def cross(d):
        z_copies[d] = pltpu.make_async_remote_copy(
            src_ref=blocks.at[d, 0],
            dst_ref=firsts.at[b, d, rows],
            send_sem=z_send.at[d],
            recv_sem=z_recv.at[d],
            device_id=other_z,
            device_id_type=MESH,
        )
        sent.append(z_copies[d])
        if d == 2:
            pl.when(b_core != farthest)(z_copies[d].start)
        else:
            z_copies[d].start()
        core_copies[d] = send(
            blocks.at[d, 0], firsts.at[b, d, rows], core_send.at[0, d], core_recv.at[0, d], other_core
        )
        own_copies[d] = pltpu.make_async_copy(blocks.at[d, 0], firsts.at[b, d, rows], own_sem.at[d])
        own_copies[d].start()

    def pass_on(d):
        z_copies[d].wait_recv()
        core_copies[5 + d].start()

    for d in range(5):
        src = firsts.at[b_z, :, tail] if d == 4 else firsts.at[b_z, d, rows]
        core_copies[5 + d] = pltpu.make_async_remote_copy(
            src_ref=src,
            dst_ref=src,
            send_sem=core_send.at[1, d],
            recv_sem=core_recv.at[1, d],
            device_id=other_core,
            device_id_type=MESH,
        )
        sent.append(core_copies[5 + d])

    fan_mine.wait()
    for copy in fans:
        copy.wait_recv()
    over_z = send(heads, heads_z, head_send.at[0], head_recv.at[0], other_half)
    cross(0)

    from_left.wait_recv()
    left_1, right_1 = ring(2, 1, 0, 2), ring(3, -1, 0, 0)
    cross(3)
    from_right.wait_recv()
    cross(1)
    over_z.wait_recv()
    over_y = send(heads_z.at[0], head_y, head_send.at[1], head_recv.at[1], along_y(3))
    left_1.wait_recv()
    from_far, far_1 = ring(4, 1, 3, 1), ring(5, -1, 1, 0)
    over_y.wait_recv()
    for d in range(4):
        place = lax.rem(x + d, 4)
        beyond = jnp.where(y == 3, jnp.zeros((LAGS, LANES), F32), head_y[...])
        after = jnp.where(place == 3, beyond, heads_z[lax.rem(place + 1, 4)])
        tails[d] = jnp.where(zh == 0, heads_z[place], after)
    z_copies[4] = send(tails, firsts.at[b, :, tail], z_send.at[4], z_recv.at[4], other_z)
    core_copies[4] = send(tails, firsts.at[b, :, tail], core_send.at[0, 4], core_recv.at[0, 4], other_core)
    own_copies[4] = pltpu.make_async_copy(tails, firsts.at[b, :, tail], own_sem.at[4])
    own_copies[4].start()
    pass_on(0)
    right_1.wait_recv()
    from_far.wait_recv()
    cross(2)
    rest = [ring(6, 1, 0, 3), ring(7, -1, 0, 1), ring(8, -1, 1, 1), ring(9, 1, 0, 0), ring(10, -1, 0, 2), ring(11, 1, 3, 0)]
    far_1.wait_recv()
    for d in (3, 1, 4):
        pass_on(d)

    def seconds(chunk):
        first, count = CHUNKS[chunk]
        for q in range(count):
            lanes = slice(q * LANES, (q + 1) * LANES)
            for d in range(4):
                for r in range(LAGS):
                    hi, lo = halves(blocks[d, first + q, pl.ds(r, PER, stride=LAGS), :])
                    to = slice(r * DEEP + d * PER, r * DEEP + (d + 1) * PER)
                    y_hi[to, lanes] = hi
                    y_lo[to, lanes] = lo

    def arrived(bb):
        @pl.when(bb == b)
        def _():
            for d in range(5):
                own_copies[d].wait()

        @pl.when(bb == b_core)
        def _():
            for d in range(5):
                core_copies[d].wait_recv()

        @pl.when(bb == b_both)
        def _():
            for d in range(5):
                core_copies[5 + d].wait_recv()

    def spread(bb):
        for m in range(1, 2 * LAGS):
            v = jnp.concatenate([firsts[bb, d, pl.ds(m, PER, stride=LAGS), :] for d in range(4)], axis=0)
            hi, lo = halves(v.T)
            lanes = slice((m - 1) * DEEP, m * DEEP)
            x_hi[bb, :, lanes] = hi
            x_lo[bb, :, lanes] = lo

    def products(chunk, e):
        bb = lax.rem(y + e, 4)
        width = WIDTHS[chunk]

        def dots(n):
            lhs_hi = jnp.concatenate(
                [x_hi[bb, :, pl.ds(pl.multiple_of(n * LEN + k * DEEP, LANES), LEN)] for k in range(LAGS)], axis=0
            )
            lhs_lo = jnp.concatenate(
                [x_lo[bb, :, pl.ds(pl.multiple_of(n * LEN + k * DEEP, LANES), LEN)] for k in range(LAGS)], axis=0
            )
            deep = pl.ds(pl.multiple_of(n * LEN, LEN), LEN)
            rhs_hi, rhs_lo = y_hi[deep, :width], y_lo[deep, :width]
            got = jnp.dot(lhs_hi, rhs_hi, preferred_element_type=F32)
            got += jnp.dot(lhs_lo, rhs_hi, preferred_element_type=F32)
            got += jnp.dot(lhs_hi, rhs_lo, preferred_element_type=F32)
            return got.reshape(2, 2, 2, LANES, width)

        def step(n, carry):
            part[chunk][e] += dots(n)
            return carry

        part[chunk][e] = dots(0)
        lax.fori_loop(1, 4, step, 0)

    fars, nears, lasts = {}, {}, {}
    ends = (1, 3)

    def near(chunk, way, u, w):
        nears[chunk, way, u, w] = send(
            part[chunk].at[ends[way], u, w],
            near_in[chunk].at[way, u, w],
            near_send.at[chunk, way, u, w],
            near_recv.at[chunk, way, u, w],
            along_y(ends[way]),
        )

    def make(chunk, e):
        if chunk == 0:
            bb = lax.rem(y + e, 4)
            if e == 2:
                pl.when(b_z == farthest)(lambda: pass_on(2))
            arrived(bb)
            if e == 2:
                pl.when(b_core == farthest)(z_copies[2].start)
            spread(bb)
        products(chunk, e)

    def sums(chunk):
        seconds(chunk)
        make(chunk, 2)
        for u in range(2):
            for way in range(2):
                fars[chunk, way, u] = send(
                    part[chunk].at[2, u, way],
                    far_in[chunk].at[way, u],
                    far_send.at[chunk, way, u],
                    far_recv.at[chunk, way, u],
                    along_y(ends[way]),
                )
        if chunk == 0:
            pl.when(b_z != farthest)(lambda: pass_on(2))
        for way in range(2):
            make(chunk, ends[way])
            for u in range(2):
                near(chunk, way, u, 1 - way)
        make(chunk, 0)

    def add_far(chunk):
        for u in range(2):
            for way in range(2):
                fars[chunk, way, u].wait_recv()
                part[chunk][ends[way], u, way] += far_in[chunk][way, u]
                near(chunk, way, u, way)

    def finish(chunk):
        for u in range(2):
            for way in range(2):
                for w in range(2):
                    nears[chunk, way, u, w].wait_recv()
            part[chunk][0, u] += near_in[chunk][0, u] + near_in[chunk][1, u]
            for other in range(2):
                zz = lax.rem(zh + other, 2)
                for row in range(2):
                    start = pl.multiple_of((zz * 2 + row) * 32, 32)
                    src = part[chunk].at[0, u, :, :, pl.ds(start, 32)]
                    dst = last_in[chunk].at[u, c, zh]
                    copy = pltpu.make_async_remote_copy(
                        src_ref=src,
                        dst_ref=dst,
                        send_sem=last_send.at[chunk, u, other, row],
                        recv_sem=last_recv.at[chunk, u, c, zh],
                        device_id=at(y, x, zz, row, zl),
                        device_id_type=MESH,
                    )
                    if other == 0:
                        here = jnp.logical_and(row == zl, zl == c)
                        own = pltpu.make_async_copy(src, dst, last_own.at[chunk, u])
                        lasts[chunk, u, row] = (here, copy, own)
                        pl.when(jnp.logical_not(here))(copy.start)
                        pl.when(here)(own.start)
                    else:
                        copy.start()
                        sent.append(copy)

    scale = [np.float32(1.0 / np.sqrt(np.float32(SAMPLES - k))) for k in range(1, LAGS + 1)]

    def write(chunk):
        first, count = CHUNKS[chunk]
        for u in range(2):
            for row in range(2):
                here, copy, own = lasts[chunk, u, row]
                pl.when(jnp.logical_not(here))(copy.wait_send)
                pl.when(here)(own.wait)
            for cc in range(2):
                for hh in range(2):
                    mine = jnp.logical_and(zl == c, jnp.logical_and(cc == c, hh == zh))
                    place = last_in[chunk].at[u, cc, hh]
                    copy = pltpu.make_async_remote_copy(
                        src_ref=place,
                        dst_ref=place,
                        send_sem=last_send.at[chunk, u, 0, 0],
                        recv_sem=last_recv.at[chunk, u, cc, hh],
                        device_id=other_z,
                        device_id_type=MESH,
                    )
                    pl.when(jnp.logical_not(mine))(copy.wait_recv)
            for cc in range(2):
                for q in range(count):
                    channels = lax.rem(x + first + q, 4)
                    lanes = pl.ds(pl.multiple_of(cc * 4 * LANES + channels * LANES, LANES), LANES)
                    piece = slice(q * LANES, (q + 1) * LANES)
                    for w in range(2):
                        for i in range(2):
                            k = u * 4 + w * 2 + i
                            total = last_in[chunk][u, cc, 0, w, i, :, piece] + last_in[chunk][u, cc, 1, w, i, :, piece]
                            out_ref[:, k, lanes] = total * scale[k]

    sums(0)
    pl.semaphore_signal(ready, inc=1, device_id=other_half, device_id_type=MESH)
    add_far(0)
    for copy in rest:
        copy.wait_recv()
    sums(1)
    pl.semaphore_wait(ready, 1)
    finish(0)
    add_far(1)
    write(0)
    finish(1)
    write(1)
    for copy in sent:
        copy.wait_send()


def shards(strain):
    dma, vmem = pltpu.SemaphoreType.DMA, pltpu.VMEM
    n = len(CHUNKS)
    return pl.pallas_call(
        kernel,
        out_shape=jax.ShapeDtypeStruct((32, LAGS, 8 * LANES), F32),
        in_specs=[pl.BlockSpec(memory_space=pl.ANY)],
        out_specs=pl.BlockSpec(memory_space=pltpu.VMEM),
        scratch_shapes=[
            vmem((4, 4, LEN, LANES), F32),
            vmem((4, 4, LEN + LAGS, LANES), F32),
            vmem((4, LAGS, LANES), F32),
            vmem((4, LAGS, LANES), F32),
            vmem((LAGS, LANES), F32),
            vmem((4, LAGS, LANES), F32),
            vmem((4, LANES, (2 * LAGS - 1) * DEEP), BF16),
            vmem((4, LANES, (2 * LAGS - 1) * DEEP), BF16),
            vmem((LAGS * DEEP, max(WIDTHS)), BF16),
            vmem((LAGS * DEEP, max(WIDTHS)), BF16),
            [vmem((4, 2, 2, 2, LANES, w), F32) for w in WIDTHS],
            [vmem((2, 2, 2, LANES, w), F32) for w in WIDTHS],
            [vmem((2, 2, 2, 2, LANES, w), F32) for w in WIDTHS],
            [vmem((2, 2, 2, 2, 2, 32, w), F32) for w in WIDTHS],
            dma((4,)), dma((5,)), dma((4,)), dma((4,)), dma((1,)), dma((2,)), dma((2,)), dma((12,)), dma((12,)),
            dma((5,)), dma((5,)), dma((2, 5)), dma((2, 5)), dma((n, 2, 2)), dma((n, 2, 2)),
            dma((n, 2, 2, 2)), dma((n, 2, 2, 2)), dma((n, 2, 2, 2)), dma((n, 2, 2, 2)), dma((n, 2)),
            pltpu.SemaphoreType.REGULAR,
        ],
        compiler_params=pltpu.CompilerParams(
            collective_id=0, has_side_effects=True, vmem_limit_bytes=60 * 2**20
        ),
        cost_estimate=pl.CostEstimate(flops=3 * 2 * 8 * 512 * 512 * 3072, bytes_accessed=2**22, transcendentals=0),
    )(strain)


def solution(mesh):
    placed = (P("tm", ("row", "col")),)
    return jax.shard_map(
        shards, mesh=mesh, in_specs=placed, out_specs=P(("tm", "row"), None, "col"), check_vma=False
    )
```

time: 941 us -> 134 us (0.14)
  the two profiles are of different devices: /device:TPU:1 before, /device:TPU:24 now
where the time goes in v2:
time: 134 us
  Pallas kernels  132 us (99%)
  local copies, waits for them, and re-layouts  2.31 us (2%)
    pallas_call x1, Pallas kernels, shards(): pl.pallas_call(kernel, out_shape=jax.ShapeDtypeStruct((32, LAGS, 8 * LANE...  132 us

profile of v2, /device:TPU:24, one launch (start us, length us, event | category | flops | bytes accessed | tf_op | source)
XLA Modules:
  0.0 134.2 jit_solution(6678984721464437727)
XLA Ops:
  0.0 131.9 %shard_map.17 = f32[32,8,1024]{2,1,0:T(8,128)} custom-call(f32[768,512]{1,0:T(8,128)} %s_ref.1), custom_call_target="tpu_custom_call" | custom-call | flops 38654705664 | bytes 4194304 | tf_op jit(solution)/shard_map/pallas_call | solution.py:361
  131.9 2.3 %copy.3 = f32[32,8,1024]{2,1,0:T(8,128)} copy(f32[32,8,1024]{2,1,0:T(8,128)} %shard_map.17) | data formatting | bytes 2097152

commit v3 on v0

v3 whole, which is shorter than its diff:
```python
import jax
import jax.numpy as jnp
import numpy as np
from jax import lax
from jax.experimental import pallas as pl
from jax.experimental.pallas import tpu as pltpu
from jax.sharding import PartitionSpec as P

MESH = pl.DeviceIdType.MESH
LAGS = 8
SAMPLES = 24576
LEN = 768
LANES = 128
PER = LEN // LAGS
DEEP = 4 * PER
WIDE = 2 * LANES
F32 = jnp.float32
BF16 = jnp.bfloat16


def halves(v):
    hi = v.astype(BF16)
    return hi, (v - hi.astype(F32)).astype(BF16)


def kernel(
    s_ref, out_ref, blocks, firsts, heads, heads_z, head_y, tails, x_hi, x_lo, y_hi, y_lo, part, swap_in, far_in, near_in, last_in,
    load_sem, own_sem, fan_send, fan_recv, fan_own, head_send, head_recv, ring_send, ring_recv, z_send, z_recv,
    core_send, core_recv, swap_send, swap_recv, far_send, far_recv, near_send, near_recv, last_send, last_recv, last_own, ready,
):
    tm, zl, c = lax.axis_index("tm"), lax.axis_index("row"), lax.axis_index("col")
    y, x, zh = lax.div(tm, 8), lax.rem(lax.div(tm, 2), 4), lax.rem(tm, 2)
    b = zl * 2 + c
    b_z, b_core, b_both = (1 - zl) * 2 + c, zl * 2 + 1 - c, (1 - zl) * 2 + 1 - c

    def at(yy, xx, zz, row, col):
        return (lax.rem(yy, 4) * 8 + lax.rem(xx, 4) * 2 + zz, row, col)

    def along_x(d):
        return at(y, x + d, zh, zl, c)

    def along_y(d):
        return at(y + d, x, zh, zl, c)

    other_z = (tm, 1 - zl, c)
    other_core = (tm, zl, 1 - c)
    other_half = at(y, x, 1 - zh, zl, c)

    barrier = pltpu.get_barrier_semaphore()
    peers = [along_x(1), along_x(3), along_x(2), along_y(1), along_y(3), other_z, other_core, other_half]
    for peer in peers:
        pl.semaphore_signal(barrier, inc=1, device_id=peer, device_id_type=MESH)

    loads = []
    for q in (1, 3, 2, 0):
        lanes = pl.ds(pl.multiple_of(lax.rem(x + q, 4) * LANES, LANES), LANES)
        loads.append(pltpu.make_async_copy(s_ref.at[:, lanes], blocks.at[0, q], load_sem.at[q]))
        loads[-1].start()
    for load in loads:
        load.wait()
    pl.semaphore_wait(barrier, len(peers))

    sent = []

    def send(src, dst, send_sem, recv_sem, device):
        copy = pltpu.make_async_remote_copy(
            src_ref=src, dst_ref=dst, send_sem=send_sem, recv_sem=recv_sem, device_id=device, device_id_type=MESH
        )
        copy.start()
        sent.append(copy)
        return copy

    whole = pl.ds(0, LEN)
    parts = (pl.ds(0, LEN // 2), pl.ds(LEN // 2, LEN // 2))

    def ring(n, way, d, q, rows=whole):
        return send(
            blocks.at[d, q, rows],
            blocks.at[(d - way) % 4, (q - way) % 4, rows],
            ring_send.at[n],
            ring_recv.at[n],
            along_x(way % 4),
        )

    fans = []
    for d in range(1, 4):
        fans.append(
            send(blocks.at[0, d, pl.ds(0, LAGS)], heads.at[x], fan_send.at[4 - d], fan_recv.at[4 - d], along_x(d))
        )
    fan_mine = pltpu.make_async_copy(blocks.at[0, 0, pl.ds(0, LAGS)], heads.at[x], fan_own.at[0])
    fan_mine.start()

    left_0, right_0 = [], []
    for h in range(2):
        left_0.append(ring(h, 1, 0, 1, parts[h]))
        right_0.append(ring(2 + h, -1, 0, 3, parts[h]))

    z_copies, core_copies, own_copies = {}, {}, {}
    tail = pl.ds(LEN, LAGS)
    farthest = lax.rem(y + 2, 4)

    def cross(d, n, rows):
        z_copies[n] = pltpu.make_async_remote_copy(
            src_ref=blocks.at[d, 0, rows],
            dst_ref=firsts.at[b, d, rows],
            send_sem=z_send.at[n],
            recv_sem=z_recv.at[n],
            device_id=other_z,
            device_id_type=MESH,
        )
        sent.append(z_copies[n])
        if d == 2:
            pl.when(b_core != farthest)(z_copies[n].start)
        else:
            z_copies[n].start()
        core_copies[n] = send(
            blocks.at[d, 0, rows], firsts.at[b, d, rows], core_send.at[0, n], core_recv.at[0, n], other_core
        )
        own_copies[n] = pltpu.make_async_copy(blocks.at[d, 0, rows], firsts.at[b, d, rows], own_sem.at[n])
        own_copies[n].start()

    def pass_on(n):
        z_copies[n].wait_recv()
        core_copies[6 + n].start()

    def late(do):
        for n in (2, 4):
            do(n)

    for n in range(6):
        d, rows = (2, parts[n // 4]) if n in (2, 4) else (n, whole)
        src = firsts.at[b_z, :, tail] if n == 5 else firsts.at[b_z, d, rows]
        core_copies[6 + n] = pltpu.make_async_remote_copy(
            src_ref=src,
            dst_ref=src,
            send_sem=core_send.at[1, n],
            recv_sem=core_recv.at[1, n],
            device_id=other_core,
            device_id_type=MESH,
        )
        sent.append(core_copies[6 + n])

    fan_mine.wait()
    for copy in fans:
        copy.wait_recv()
    over_z = send(heads, heads_z, head_send.at[0], head_recv.at[0], other_half)
    cross(0, 0, whole)

    def seconds(first, q, d):
        cols = slice(q * LANES, (q + 1) * LANES)
        for r in range(LAGS):
            hi, lo = halves(blocks[d, first + q, pl.ds(r, PER, stride=LAGS), :])
            to = pl.ds(pl.multiple_of(r * DEEP + d * PER, PER), PER)
            y_hi[to, cols] = hi
            y_lo[to, cols] = lo

    left_0[0].wait_recv()
    right_0[0].wait_recv()
    left_1, right_1, from_far, far_1 = [], [], [], []
    for h in range(2):
        left_1.append(ring(4 + h, 1, 0, 2, parts[h]))
        right_1.append(ring(6 + h, -1, 0, 0, parts[h]))
    left_0[1].wait_recv()
    cross(3, 3, whole)
    right_0[1].wait_recv()
    cross(1, 1, whole)
    over_z.wait_recv()
    over_y = send(heads_z.at[0], head_y, head_send.at[1], head_recv.at[1], along_y(3))
    seconds(0, 0, 0)
    seconds(0, 1, 0)
    for h in range(2):
        left_1[h].wait_recv()
        from_far.append(ring(8 + h, 1, 3, 1, parts[h]))
        far_1.append(ring(10 + h, -1, 1, 0, parts[h]))
    over_y.wait_recv()
    for d in range(4):
        place = lax.rem(x + d, 4)
        beyond = jnp.where(y == 3, jnp.zeros((LAGS, LANES), F32), head_y[...])
        after = jnp.where(place == 3, beyond, heads_z[lax.rem(place + 1, 4)])
        tails[d] = jnp.where(zh == 0, heads_z[place], after)
    z_copies[5] = send(tails, firsts.at[b, :, tail], z_send.at[5], z_recv.at[5], other_z)
    core_copies[5] = send(tails, firsts.at[b, :, tail], core_send.at[0, 5], core_recv.at[0, 5], other_core)
    own_copies[5] = pltpu.make_async_copy(tails, firsts.at[b, :, tail], own_sem.at[5])
    own_copies[5].start()
    pass_on(0)
    for h in range(2):
        right_1[h].wait_recv()
    seconds(0, 0, 3)
    seconds(0, 1, 3)
    seconds(0, 0, 1)
    seconds(0, 1, 1)
    for h in range(2):
        from_far[h].wait_recv()
        cross(2, 2 + 2 * h, parts[h])
    rest = [ring(12, 1, 0, 3), ring(13, -1, 0, 1), ring(14, -1, 1, 1), ring(15, 1, 0, 0), ring(16, -1, 0, 2), ring(17, 1, 3, 0)]
    for h in range(2):
        far_1[h].wait_recv()
    seconds(0, 0, 2)
    seconds(0, 1, 2)
    for n in (3, 1, 5):
        pass_on(n)

    def arrived(bb):
        @pl.when(bb == b)
        def _():
            for n in range(6):
                own_copies[n].wait()

        @pl.when(bb == b_core)
        def _():
            for n in range(6):
                core_copies[n].wait_recv()

        @pl.when(bb == b_both)
        def _():
            for n in range(6):
                core_copies[6 + n].wait_recv()

    def spread(bb):
        for m in range(1, 2 * LAGS):
            v = jnp.concatenate([firsts[bb, d, pl.ds(m, PER, stride=LAGS), :] for d in range(4)], axis=0)
            hi, lo = halves(v.T)
            lanes = slice((m - 1) * DEEP, m * DEEP)
            x_hi[bb, :, lanes] = hi
            x_lo[bb, :, lanes] = lo

    ends = (1, 3)
    lanes = (pl.ds(0, LANES), pl.ds(LANES, LANES))
    mine = pl.ds(pl.multiple_of(zh * 64, 64), 64)
    yours = pl.ds(pl.multiple_of((1 - zh) * 64, 64), 64)
    span = (pl.ds(0, LANES), mine)

    def remote(src, dst, send_sem, recv_sem, device):
        return pltpu.make_async_remote_copy(
            src_ref=src, dst_ref=dst, send_sem=send_sem, recv_sem=recv_sem, device_id=device, device_id_type=MESH
        )

    def swap(chunk, e, n):
        if e in ends:
            src, dst = part.at[chunk, e, :, n, :, yours, lanes[1]], swap_in.at[chunk, e, :, n]
        else:
            src, dst = part.at[chunk, e, n, :, :, yours, lanes[1]], swap_in.at[chunk, e, n]
        return remote(src, dst, swap_send.at[chunk, e, n], swap_recv.at[chunk, e, n], other_half)

    def add_swap(chunk, e, n):
        swap(chunk, e, n).wait_recv()
        if e in ends:
            part[chunk, e, :, n, :, mine, lanes[1]] += swap_in[chunk, e, :, n]
        else:
            part[chunk, e, n, :, :, mine, lanes[1]] += swap_in[chunk, e, n]

    def far(chunk, f, way, u):
        return remote(
            part.at[chunk, 2, u, way, :, span[f], lanes[f]],
            far_in[f].at[chunk, way, u],
            far_send.at[chunk, f, way, u],
            far_recv.at[chunk, f, way, u],
            along_y(ends[way]),
        )

    def near(chunk, f, way, u, w):
        return remote(
            part.at[chunk, ends[way], u, w, :, span[f], lanes[f]],
            near_in[f].at[chunk, way, u, w],
            near_send.at[chunk, f, way, u, w],
            near_recv.at[chunk, f, way, u, w],
            along_y(ends[way]),
        )

    def pure(chunk, f, way):
        for u in range(2):
            near(chunk, f, way, u, 1 - way).start()

    def add_far(chunk, f):
        for u in range(2):
            for way in range(2):
                far(chunk, f, way, u).wait_recv()
                part[chunk, ends[way], u, way, :, span[f], lanes[f]] += far_in[f][chunk, way, u]
                near(chunk, f, way, u, way).start()

    def after(chunk, j):
        if j < 2:
            swap(chunk, 2, j).start()
            for way in range(2):
                far(chunk, 0, way, j).start()
        elif j < 6:
            way = j % 2
            n = 1 - way if j < 4 else way
            swap(chunk, ends[way], n).start()
            if j < 4:
                pure(chunk, 0, way)
        else:
            swap(chunk, 0, j - 6).start()
        if j == 3:
            for u in range(2):
                add_swap(chunk, 2, u)
                for way in range(2):
                    far(chunk, 1, way, u).start()
        if j == 5:
            add_far(chunk, 0)
            for way in range(2):
                add_swap(chunk, ends[way], 1 - way)
                pure(chunk, 1, way)
        if j == 7:
            for way in range(2):
                add_swap(chunk, ends[way], way)
            add_far(chunk, 1)

    def before(s):
        if s == 0:
            pl.when(b_z == farthest)(lambda: late(pass_on))
            arrived(farthest)
            pl.when(b_core == farthest)(lambda: late(lambda n: z_copies[n].start()))
        if s == 2:
            pl.when(b_z != farthest)(lambda: late(pass_on))
            arrived(lax.rem(y + 1, 4))
        if s == 3:
            arrived(lax.rem(y + 3, 4))
        if s == 6:
            arrived(y)
        if s == 8:
            pl.semaphore_signal(ready, inc=1, device_id=other_half, device_id_type=MESH)
            for copy in rest:
                copy.wait_recv()

            def one(d, carry):
                for q in range(2):
                    seconds(2, q, d)
                return carry

            lax.fori_loop(0, 4, one, 0)

    def step(s, carry):
        chunk, j = lax.div(s, 8), lax.rem(s, 8)
        odd = lax.rem(j, 2)
        e = jnp.where(j < 2, 2, jnp.where(j < 6, 1 + 2 * odd, 0))
        bb = lax.rem(y + e, 4)
        for i in (0, 2, 3, 6, 8):
            pl.when(s == i)(lambda i=i: before(i))
        pl.when(jnp.logical_or(s == 0, jnp.logical_or(jnp.logical_or(s == 2, s == 3), s == 6)))(lambda: spread(bb))

        by_way = jnp.logical_and(j >= 2, j < 6)
        w = jnp.where(j < 4, 1 - odd, odd)
        pairs = [
            (jnp.where(by_way, 0, odd), jnp.where(by_way, w, 0)),
            (jnp.where(by_way, 1, odd), jnp.where(by_way, w, 1)),
        ]
        for u, w in pairs:
            pass

        def dots(n, carry):
            starts = [
                pl.multiple_of( (u * 4 + w * 2 + i) * DEEP, LANES) for u, w in pairs for i in range(2)
            ]
            lhs_hi = jnp.concatenate([x_hi[bb, :, pl.ds(start, LAGS * DEEP)] for start in starts], axis=0)
            lhs_lo = jnp.concatenate([x_lo[bb, :, pl.ds(start, LAGS * DEEP)] for start in starts], axis=0)
            deep = pl.ds(0, LAGS * DEEP)
            rhs_hi, rhs_lo = y_hi[deep, :], y_lo[deep, :]
            got = jnp.dot(lhs_hi, rhs_hi, preferred_element_type=F32)
            got += jnp.dot(lhs_lo, rhs_hi, preferred_element_type=F32)
            got += jnp.dot(lhs_hi, rhs_lo, preferred_element_type=F32)
            got = got.reshape(2, 2, LANES, WIDE)
            for n, (u, w) in enumerate(pairs):
                part[chunk, e, u, w] = got[n]
            return carry

        dots(0, 0)
        for i in range(8):
            pl.when(j == i)(lambda i=i: after(chunk, i))

        @pl.when(s == 10)
        def _():
            pl.semaphore_wait(ready, 1)
            finish(0, 0)
            finish(0, 1)

        return carry

    def total(chunk, f, u):
        for way in range(2):
            for w in range(2):
                near(chunk, f, way, u, w).wait_recv()
        part[chunk, 0, u, :, :, span[f], lanes[f]] += near_in[f][chunk, 0, u] + near_in[f][chunk, 1, u]

    def deal(chunk, f, u, other, row):
        zz = lax.rem(zh + other, 2)
        src = part.at[chunk, 0, u, :, :, pl.ds(pl.multiple_of((zz * 2 + row) * 32, 32), 32), lanes[f]]
        dst = last_in[0].at[chunk, u, c, zh] if f == 0 else last_in[1].at[chunk, u, c]
        recv_sem = last_recv.at[chunk, u, c, zh] if f == 0 else last_recv.at[chunk, u, c, 2]
        copy = remote(src, dst, last_send.at[chunk, f, u, other, row], recv_sem, at(y, x, zz, row, zl))
        return copy, pltpu.make_async_copy(src, dst, last_own.at[chunk, f, u]) if other == 0 else None

    def finish(chunk, f):
        for u in range(2):
            if f == 1:
                add_swap(chunk, 0, u)
            total(chunk, f, u)
            for other in range(2 - f):
                for row in range(2):
                    copy, own = deal(chunk, f, u, other, row)
                    if other == 0:
                        here = jnp.logical_and(row == zl, zl == c)
                        pl.when(jnp.logical_not(here))(copy.start)
                        pl.when(here)(own.start)
                    else:
                        copy.start()

    scale = [np.float32(1.0 / np.sqrt(np.float32(SAMPLES - k))) for k in range(1, LAGS + 1)]

    def write(chunk, f):
        channels = lax.rem(x + 2 * chunk + f, 4)
        for u in range(2):
            for other in range(2 - f):
                for row in range(2):
                    copy, own = deal(chunk, f, u, other, row)
                    if other == 0:
                        here = jnp.logical_and(row == zl, zl == c)
                        pl.when(jnp.logical_not(here))(copy.wait_send)
                        pl.when(here)(own.wait)
                    else:
                        copy.wait_send()
            for cc in range(2):
                for hh in range(2) if f == 0 else (2,):
                    same = jnp.logical_and(zl == c, cc == c)
                    if f == 0:
                        same = jnp.logical_and(same, hh == zh)
                    place = last_in[0].at[chunk, u, cc, hh] if f == 0 else last_in[1].at[chunk, u, cc]
                    copy = pltpu.make_async_remote_copy(
                        src_ref=place,
                        dst_ref=place,
                        send_sem=last_send.at[chunk, f, u, 0, 0],
                        recv_sem=last_recv.at[chunk, u, cc, hh],
                        device_id=other_z,
                        device_id_type=MESH,
                    )
                    pl.when(jnp.logical_not(same))(copy.wait_recv)
            for cc in range(2):
                to = pl.ds(pl.multiple_of(cc * 4 * LANES + channels * LANES, LANES), LANES)
                for w in range(2):
                    for i in range(2):
                        k = u * 4 + w * 2 + i
                        if f == 0:
                            got = last_in[0][chunk, u, cc, 0, w, i] + last_in[0][chunk, u, cc, 1, w, i]
                        else:
                            got = last_in[1][chunk, u, cc, w, i]
                        out_ref[:, k, to] = got * scale[k]

    lax.fori_loop(0, 16, step, 0)
    finish(1, 0)
    write(0, 0)
    write(0, 1)
    finish(1, 1)
    write(1, 0)
    write(1, 1)
    for copy in sent:
        copy.wait_send()

    def drain(chunk, carry):
        for n in range(2):
            for e in range(4):
                swap(chunk, e, n).wait_send()
        for f in range(2):
            for way in range(2):
                for u in range(2):
                    far(chunk, f, way, u).wait_send()
                    for w in range(2):
                        near(chunk, f, way, u, w).wait_send()
        return carry

    lax.fori_loop(0, 2, drain, 0)


def shards(strain):
    dma, vmem = pltpu.SemaphoreType.DMA, pltpu.VMEM
    return pl.pallas_call(
        kernel,
        out_shape=jax.ShapeDtypeStruct((32, LAGS, 8 * LANES), F32),
        in_specs=[pl.BlockSpec(memory_space=pl.ANY)],
        out_specs=pl.BlockSpec(memory_space=pltpu.VMEM),
        scratch_shapes=[
            vmem((4, 4, LEN, LANES), F32),
            vmem((4, 4, LEN + LAGS, LANES), F32),
            vmem((4, LAGS, LANES), F32),
            vmem((4, LAGS, LANES), F32),
            vmem((LAGS, LANES), F32),
            vmem((4, LAGS, LANES), F32),
            vmem((4, LANES, (2 * LAGS - 1) * DEEP), BF16),
            vmem((4, LANES, (2 * LAGS - 1) * DEEP), BF16),
            vmem((LAGS * DEEP, WIDE), BF16),
            vmem((LAGS * DEEP, WIDE), BF16),
            vmem((2, 4, 2, 2, 2, LANES, WIDE), F32),
            vmem((2, 4, 2, 2, 2, 64, LANES), F32),
            [vmem((2, 2, 2, 2, n, LANES), F32) for n in (LANES, 64)],
            [vmem((2, 2, 2, 2, 2, n, LANES), F32) for n in (LANES, 64)],
            [vmem((2, 2, 2, 2, 2, 2, 32, LANES), F32), vmem((2, 2, 2, 2, 2, 32, LANES), F32)],
            dma((4,)), dma((6,)), dma((4,)), dma((4,)), dma((1,)), dma((2,)), dma((2,)), dma((18,)), dma((18,)),
            dma((6,)), dma((6,)), dma((2, 6)), dma((2, 6)), dma((2, 4, 2)), dma((2, 4, 2)),
            dma((2, 2, 2, 2)), dma((2, 2, 2, 2)), dma((2, 2, 2, 2, 2)), dma((2, 2, 2, 2, 2)),
            dma((2, 2, 2, 2, 2)), dma((2, 2, 2, 3)), dma((2, 2, 2)),
            pltpu.SemaphoreType.REGULAR,
        ],
        compiler_params=pltpu.CompilerParams(
            collective_id=0, has_side_effects=True, vmem_limit_bytes=60 * 2**20
        ),
        cost_estimate=pl.CostEstimate(flops=3 * 2 * 8 * 512 * 512 * 3072, bytes_accessed=2**22, transcendentals=0),
    )(strain)


def solution(mesh):
    placed = (P("tm", ("row", "col")),)
    return jax.shard_map(
        shards, mesh=mesh, in_specs=placed, out_specs=P(("tm", "row"), None, "col"), check_vma=False
    )
```

time: 941 us -> 124 us (0.13)
  waiting for transfers between devices: 787 us -> 0 us
  Pallas kernels: 0 us -> 121 us
  matrix products: 97.5 us -> 0 us
  local copies, waits for them, and re-layouts: 26.9 us -> 2.31 us
  between operations: 13.7 us -> 0.01 us
    reduce_scatter x1 -> x0, waiting for transfers between devices: 714 us -> none  [shards(): return lax.psum_scatter(terms, 'tm', scatter_dimension=0, tiled=True)]
    pallas_call x0 -> x1, Pallas kernels: none -> 121 us  [shards(): pl.pallas_call(kernel, out_shape=jax.ShapeDtypeStruct((32, LAGS, 8 * LANE...]
    dot_general x8 -> x0, matrix products: 97.5 us -> none  [shards(): jnp.einsum('ti,tj->ij', lagged, col_panel, precision=lax.Precision.HIGHES...]
    all_gather x1 -> x0, waiting for transfers between devices: 67.8 us -> none  [shards(): whole = lax.all_gather(strain, ('row', 'col'), axis=1, tiled=True)]
    slice x3 -> x0, local copies, waits for them, and re-layouts: 20.7 us -> none  [the longest x1 19.1 us: shards(): lagged = row_panel[lag:lag + length]]
  transfers between devices with their start and end apart: 3 -> 0, of which waited for: 3 -> 0; matrix products, arithmetic and copies ran while one was open for 0% -> 0% of each run, Pallas kernels for 0% -> 0%
where the time goes in v3:
time: 124 us
  Pallas kernels  121 us (98%)
  local copies, waits for them, and re-layouts  2.31 us (2%)
    pallas_call x1, Pallas kernels, shards(): pl.pallas_call(kernel, out_shape=jax.ShapeDtypeStruct((32, LAGS, 8 * LANE...  121 us

profile of v3, /device:TPU:1, one launch (start us, length us, event | category | flops | bytes accessed | tf_op | source)
XLA Modules:
  0.0 123.6 jit_solution(8475886761097229700)
XLA Ops:
  0.0 121.2 %shard_map.17 = f32[32,8,1024]{2,1,0:T(8,128)} custom-call(f32[768,512]{1,0:T(8,128)} %s_ref.1), custom_call_target="tpu_custom_call" | custom-call | flops 38654705664 | bytes 4194304 | tf_op jit(solution)/shard_map/pallas_call | solution.py:475
  121.2 2.3 %copy.3 = f32[32,8,1024]{2,1,0:T(8,128)} copy(f32[32,8,1024]{2,1,0:T(8,128)} %shard_map.17) | data formatting | bytes 2097152

commit v4 on v3

--- a/solution.py
+++ b/solution.py
@@ -14,6 +14,7 @@
 PER = LEN // LAGS
 DEEP = 4 * PER
 WIDE = 2 * LANES
+STRAIGHT = ((1, 1),)
 F32 = jnp.float32
 BF16 = jnp.bfloat16
 
@@ -98,6 +99,8 @@
     z_copies, core_copies, own_copies = {}, {}, {}
     tail = pl.ds(LEN, LAGS)
     farthest = lax.rem(y + 2, 4)
+    later = jnp.logical_or(b_core == farthest, b == y)
+    later_z = jnp.logical_or(b_both == farthest, b_z == y)
 
     def cross(d, n, rows):
         z_copies[n] = pltpu.make_async_remote_copy(
@@ -110,7 +113,7 @@
         )
         sent.append(z_copies[n])
         if d == 2:
-            pl.when(b_core != farthest)(z_copies[n].start)
+            pl.when(jnp.logical_not(later))(z_copies[n].start)
         else:
             z_copies[n].start()
         core_copies[n] = send(
@@ -228,96 +231,110 @@
     lanes = (pl.ds(0, LANES), pl.ds(LANES, LANES))
     mine = pl.ds(pl.multiple_of(zh * 64, 64), 64)
     yours = pl.ds(pl.multiple_of((1 - zh) * 64, 64), 64)
-    span = (pl.ds(0, LANES), mine)
 
     def remote(src, dst, send_sem, recv_sem, device):
         return pltpu.make_async_remote_copy(
             src_ref=src, dst_ref=dst, send_sem=send_sem, recv_sem=recv_sem, device_id=device, device_id_type=MESH
         )
 
+    def whole_sums(chunk, f, u):
+        return f == 0 or (chunk, u) in STRAIGHT
+
     def swap(chunk, e, n):
-        if e in ends:
+        if e not in ends:
+            src, dst = part.at[chunk, e, n, :, :, yours, lanes[1]], swap_in.at[chunk, e, n]
+        elif whole_sums(chunk, 1, 1):
+            src, dst = part.at[chunk, e, 0, n, :, yours, lanes[1]], swap_in.at[chunk, e, 0, n]
+        else:
             src, dst = part.at[chunk, e, :, n, :, yours, lanes[1]], swap_in.at[chunk, e, :, n]
-        else:
-            src, dst = part.at[chunk, e, n, :, :, yours, lanes[1]], swap_in.at[chunk, e, n]
         return remote(src, dst, swap_send.at[chunk, e, n], swap_recv.at[chunk, e, n], other_half)
 
     def add_swap(chunk, e, n):
         swap(chunk, e, n).wait_recv()
-        if e in ends:
+        if e not in ends:
+            part[chunk, e, n, :, :, mine, lanes[1]] += swap_in[chunk, e, n]
+        elif whole_sums(chunk, 1, 1):
+            part[chunk, e, 0, n, :, mine, lanes[1]] += swap_in[chunk, e, 0, n]
+        else:
             part[chunk, e, :, n, :, mine, lanes[1]] += swap_in[chunk, e, :, n]
-        else:
-            part[chunk, e, n, :, :, mine, lanes[1]] += swap_in[chunk, e, n]
+
+    def span(chunk, f, u):
+        return (pl.ds(0, LANES), pl.ds(0, LANES)) if whole_sums(chunk, f, u) else (mine, pl.ds(0, 64))
 
     def far(chunk, f, way, u):
+        here, there = span(chunk, f, u)
         return remote(
-            part.at[chunk, 2, u, way, :, span[f], lanes[f]],
-            far_in[f].at[chunk, way, u],
+            part.at[chunk, 2, u, way, :, here, lanes[f]],
+            far_in.at[chunk, f, way, u, :, there],
             far_send.at[chunk, f, way, u],
             far_recv.at[chunk, f, way, u],
             along_y(ends[way]),
         )
 
     def near(chunk, f, way, u, w):
+        here, there = span(chunk, f, u)
         return remote(
-            part.at[chunk, ends[way], u, w, :, span[f], lanes[f]],
-            near_in[f].at[chunk, way, u, w],
+            part.at[chunk, ends[way], u, w, :, here, lanes[f]],
+            near_in.at[chunk, f, way, u, w, :, there],
             near_send.at[chunk, f, way, u, w],
             near_recv.at[chunk, f, way, u, w],
             along_y(ends[way]),
         )
 
-    def pure(chunk, f, way):
-        for u in range(2):
-            near(chunk, f, way, u, 1 - way).start()
-
-    def add_far(chunk, f):
-        for u in range(2):
+    def kinds(chunk, straight):
+        return [(f, u) for f in range(2) for u in range(2) if whole_sums(chunk, f, u) == straight]
+
+    def add_far(chunk, straight):
+        for f, u in kinds(chunk, straight):
+            here, there = span(chunk, f, u)
             for way in range(2):
                 far(chunk, f, way, u).wait_recv()
-                part[chunk, ends[way], u, way, :, span[f], lanes[f]] += far_in[f][chunk, way, u]
+                part[chunk, ends[way], u, way, :, here, lanes[f]] += far_in[chunk, f, way, u, :, there]
                 near(chunk, f, way, u, way).start()
 
-    def after(chunk, j):
+    def after_product(chunk, j):
         if j < 2:
-            swap(chunk, 2, j).start()
-            for way in range(2):
-                far(chunk, 0, way, j).start()
+            for f, u in kinds(chunk, True):
+                if u == j:
+                    for way in range(2):
+                        far(chunk, f, way, u).start()
+            if not whole_sums(chunk, 1, j):
+                swap(chunk, 2, j).start()
         elif j < 6:
             way = j % 2
             n = 1 - way if j < 4 else way
+            if j < 4:
+                for f, u in kinds(chunk, True):
+                    near(chunk, f, way, u, 1 - way).start()
             swap(chunk, ends[way], n).start()
-            if j < 4:
-                pure(chunk, 0, way)
-        else:
+        elif not whole_sums(chunk, 1, j - 6):
             swap(chunk, 0, j - 6).start()
-        if j == 3:
-            for u in range(2):
+
+    def after_step(chunk, p):
+        if p == 4:
+            for f, u in kinds(chunk, False):
                 add_swap(chunk, 2, u)
                 for way in range(2):
-                    far(chunk, 1, way, u).start()
-        if j == 5:
-            add_far(chunk, 0)
+                    far(chunk, f, way, u).start()
+        if p == 5:
+            add_far(chunk, True)
+        if p == 6:
             for way in range(2):
                 add_swap(chunk, ends[way], 1 - way)
-                pure(chunk, 1, way)
-        if j == 7:
+                for f, u in kinds(chunk, False):
+                    near(chunk, f, way, u, 1 - way).start()
+        if p == 7:
             for way in range(2):
                 add_swap(chunk, ends[way], way)
-            add_far(chunk, 1)
+            add_far(chunk, False)
 
     def before(s):
-        if s == 0:
-            pl.when(b_z == farthest)(lambda: late(pass_on))
-            arrived(farthest)
-            pl.when(b_core == farthest)(lambda: late(lambda n: z_copies[n].start()))
+        if s == 1:
+            pl.when(later)(lambda: late(lambda n: z_copies[n].start()))
         if s == 2:
-            pl.when(b_z != farthest)(lambda: late(pass_on))
-            arrived(lax.rem(y + 1, 4))
-        if s == 3:
-            arrived(lax.rem(y + 3, 4))
-        if s == 6:
-            arrived(y)
+            pl.when(jnp.logical_not(later_z))(lambda: late(pass_on))
+        if s == 4:
+            pl.when(later_z)(lambda: late(pass_on))
         if s == 8:
             pl.semaphore_signal(ready, inc=1, device_id=other_half, device_id_type=MESH)
             for copy in rest:
@@ -330,14 +347,29 @@
 
             lax.fori_loop(0, 4, one, 0)
 
+    far_here = zl == lax.div(farthest, 2)
+    near_first = jnp.where(far_here, 1 - lax.rem(y, 2), lax.rem(y, 2))
+
     def step(s, carry):
-        chunk, j = lax.div(s, 8), lax.rem(s, 8)
+        chunk, p = lax.div(s, 8), lax.rem(s, 8)
+        by_far = jnp.logical_or(far_here, chunk == 1)
+        second = lax.rem(p, 2)
+        near_l = jnp.where(p < 4, 2, 4) + jnp.where(second == 0, near_first, 1 - near_first)
+        near_r = jnp.where(p < 2, near_first, 1 - near_first) + 2 * second + 2
+        order_l = jnp.where(jnp.logical_and(p >= 2, p < 6), near_l, p)
+        order_r = jnp.where(p >= 6, p, jnp.where(jnp.logical_and(p >= 2, p < 4), p - 2, near_r))
+        j = jnp.where(by_far, order_l, order_r)
         odd = lax.rem(j, 2)
         e = jnp.where(j < 2, 2, jnp.where(j < 6, 1 + 2 * odd, 0))
         bb = lax.rem(y + e, 4)
-        for i in (0, 2, 3, 6, 8):
+        for i in (1, 2, 4, 8):
             pl.when(s == i)(lambda i=i: before(i))
-        pl.when(jnp.logical_or(s == 0, jnp.logical_or(jnp.logical_or(s == 2, s == 3), s == 6)))(lambda: spread(bb))
+        fresh = jnp.logical_or(jnp.logical_or(s == 0, s == 2), jnp.logical_or(s == 6, s == jnp.where(far_here, 3, 4)))
+
+        @pl.when(fresh)
+        def _():
+            arrived(bb)
+            spread(bb)
 
         by_way = jnp.logical_and(j >= 2, j < 6)
         w = jnp.where(j < 4, 1 - odd, odd)
@@ -365,8 +397,10 @@
             return carry
 
         dots(0, 0)
-        for i in range(8):
-            pl.when(j == i)(lambda i=i: after(chunk, i))
+        for i in range(16):
+            pl.when(jnp.logical_and(chunk == i // 8, j == i % 8))(lambda i=i: after_product(i // 8, i % 8))
+        for i in (4, 5, 6, 7, 12, 13, 14, 15):
+            pl.when(s == i)(lambda i=i: after_step(i // 8, i % 8))
 
         @pl.when(s == 10)
         def _():
@@ -377,61 +411,67 @@
         return carry
 
     def total(chunk, f, u):
+        here, there = span(chunk, f, u)
         for way in range(2):
             for w in range(2):
                 near(chunk, f, way, u, w).wait_recv()
-        part[chunk, 0, u, :, :, span[f], lanes[f]] += near_in[f][chunk, 0, u] + near_in[f][chunk, 1, u]
-
-    def deal(chunk, f, u, other, row):
-        zz = lax.rem(zh + other, 2)
-        src = part.at[chunk, 0, u, :, :, pl.ds(pl.multiple_of((zz * 2 + row) * 32, 32), 32), lanes[f]]
-        dst = last_in[0].at[chunk, u, c, zh] if f == 0 else last_in[1].at[chunk, u, c]
-        recv_sem = last_recv.at[chunk, u, c, zh] if f == 0 else last_recv.at[chunk, u, c, 2]
-        copy = remote(src, dst, last_send.at[chunk, f, u, other, row], recv_sem, at(y, x, zz, row, zl))
-        return copy, pltpu.make_async_copy(src, dst, last_own.at[chunk, f, u]) if other == 0 else None
-
-    def finish(chunk, f):
-        for u in range(2):
-            if f == 1:
+        part[chunk, 0, u, :, :, here, lanes[f]] += (
+            near_in[chunk, f, 0, u, :, :, there] + near_in[chunk, f, 1, u, :, :, there]
+        )
+
+    def deals(chunk, f, u):
+        straight = whole_sums(chunk, f, u)
+        half = zh if straight else 0
+        for other in range(2 if straight else 1):
+            for row in range(2):
+                zz = lax.rem(zh + other, 2)
+                src = part.at[chunk, 0, u, :, :, pl.ds(pl.multiple_of((zz * 2 + row) * 32, 32), 32), lanes[f]]
+                dst = last_in.at[chunk, f, u, c, half]
+                copy = remote(
+                    src,
+                    dst,
+                    last_send.at[chunk, f, u, other, row],
+                    last_recv.at[chunk, f, u, c, half],
+                    at(y, x, zz, row, zl),
+                )
+                if other == 0:
+                    here = jnp.logical_and(row == zl, zl == c)
+                    yield here, copy, pltpu.make_async_copy(src, dst, last_own.at[chunk, f, u])
+                else:
+                    yield None, copy, None
+
+    def finish(chunk, f, units=(0, 1)):
+        for u in units:
+            if not whole_sums(chunk, f, u):
                 add_swap(chunk, 0, u)
             total(chunk, f, u)
-            for other in range(2 - f):
-                for row in range(2):
-                    copy, own = deal(chunk, f, u, other, row)
-                    if other == 0:
-                        here = jnp.logical_and(row == zl, zl == c)
-                        pl.when(jnp.logical_not(here))(copy.start)
-                        pl.when(here)(own.start)
-                    else:
-                        copy.start()
+            for here, copy, own in deals(chunk, f, u):
+                if here is None:
+                    copy.start()
+                else:
+                    pl.when(jnp.logical_not(here))(copy.start)
+                    pl.when(here)(own.start)
 
     scale = [np.float32(1.0 / np.sqrt(np.float32(SAMPLES - k))) for k in range(1, LAGS + 1)]
 
-    def write(chunk, f):
+    def write(chunk, f, units=(0, 1)):
         channels = lax.rem(x + 2 * chunk + f, 4)
-        for u in range(2):
-            for other in range(2 - f):
-                for row in range(2):
-                    copy, own = deal(chunk, f, u, other, row)
-                    if other == 0:
-                        here = jnp.logical_and(row == zl, zl == c)
-                        pl.when(jnp.logical_not(here))(copy.wait_send)
-                        pl.when(here)(own.wait)
-                    else:
-                        copy.wait_send()
+        for u in units:
+            for here, copy, own in deals(chunk, f, u):
+                if here is None:
+                    copy.wait_send()
+                else:
+                    pl.when(jnp.logical_not(here))(copy.wait_send)
+                    pl.when(here)(own.wait)
+            straight = whole_sums(chunk, f, u)
             for cc in range(2):
-                for hh in range(2) if f == 0 else (2,):
+                for hh in range(2 if straight else 1):
                     same = jnp.logical_and(zl == c, cc == c)
-                    if f == 0:
+                    if straight:
                         same = jnp.logical_and(same, hh == zh)
-                    place = last_in[0].at[chunk, u, cc, hh] if f == 0 else last_in[1].at[chunk, u, cc]
-                    copy = pltpu.make_async_remote_copy(
-                        src_ref=place,
-                        dst_ref=place,
-                        send_sem=last_send.at[chunk, f, u, 0, 0],
-                        recv_sem=last_recv.at[chunk, u, cc, hh],
-                        device_id=other_z,
-                        device_id_type=MESH,
+                    place = last_in.at[chunk, f, u, cc, hh]
+                    copy = remote(
+                        place, place, last_send.at[chunk, f, u, 0, 0], last_recv.at[chunk, f, u, cc, hh], other_z
                     )
                     pl.when(jnp.logical_not(same))(copy.wait_recv)
             for cc in range(2):
@@ -439,35 +479,32 @@
                 for w in range(2):
                     for i in range(2):
                         k = u * 4 + w * 2 + i
-                        if f == 0:
-                            got = last_in[0][chunk, u, cc, 0, w, i] + last_in[0][chunk, u, cc, 1, w, i]
-                        else:
-                            got = last_in[1][chunk, u, cc, w, i]
+                        got = last_in[chunk, f, u, cc, 0, w, i]
+                        if straight:
+                            got += last_in[chunk, f, u, cc, 1, w, i]
                         out_ref[:, k, to] = got * scale[k]
 
     lax.fori_loop(0, 16, step, 0)
-    finish(1, 0)
     write(0, 0)
     write(0, 1)
-    finish(1, 1)
+    finish(1, 0)
+    finish(1, 1, (1, 0))
     write(1, 0)
-    write(1, 1)
+    write(1, 1, (1, 0))
     for copy in sent:
         copy.wait_send()
 
-    def drain(chunk, carry):
+    for chunk in range(2):
         for n in range(2):
             for e in range(4):
-                swap(chunk, e, n).wait_send()
+                if e in ends or not whole_sums(chunk, 1, n):
+                    swap(chunk, e, n).wait_send()
         for f in range(2):
             for way in range(2):
                 for u in range(2):
                     far(chunk, f, way, u).wait_send()
                     for w in range(2):
                         near(chunk, f, way, u, w).wait_send()
-        return carry
-
-    lax.fori_loop(0, 2, drain, 0)
 
 
 def shards(strain):
@@ -490,13 +527,13 @@
             vmem((LAGS * DEEP, WIDE), BF16),
             vmem((2, 4, 2, 2, 2, LANES, WIDE), F32),
             vmem((2, 4, 2, 2, 2, 64, LANES), F32),
-            [vmem((2, 2, 2, 2, n, LANES), F32) for n in (LANES, 64)],
-            [vmem((2, 2, 2, 2, 2, n, LANES), F32) for n in (LANES, 64)],
-            [vmem((2, 2, 2, 2, 2, 2, 32, LANES), F32), vmem((2, 2, 2, 2, 2, 32, LANES), F32)],
+            vmem((2, 2, 2, 2, 2, LANES, LANES), F32),
+            vmem((2, 2, 2, 2, 2, 2, LANES, LANES), F32),
+            vmem((2, 2, 2, 2, 2, 2, 2, 32, LANES), F32),
             dma((4,)), dma((6,)), dma((4,)), dma((4,)), dma((1,)), dma((2,)), dma((2,)), dma((18,)), dma((18,)),
             dma((6,)), dma((6,)), dma((2, 6)), dma((2, 6)), dma((2, 4, 2)), dma((2, 4, 2)),
             dma((2, 2, 2, 2)), dma((2, 2, 2, 2)), dma((2, 2, 2, 2, 2)), dma((2, 2, 2, 2, 2)),
-            dma((2, 2, 2, 2, 2)), dma((2, 2, 2, 3)), dma((2, 2, 2)),
+            dma((2, 2, 2, 2, 2)), dma((2, 2, 2, 2, 2)), dma((2, 2, 2)),
             pltpu.SemaphoreType.REGULAR,
         ],
         compiler_params=pltpu.CompilerParams(

time: 124 us -> 118 us (0.952)
  Pallas kernels: 121 us -> 115 us
    pallas_call x1, Pallas kernels: 121 us -> 115 us  [shards(): pl.pallas_call(kernel, out_shape=jax.ShapeDtypeStruct((32, LAGS, 8 * LANE...]
where the time goes in v4:
time: 118 us
  Pallas kernels  115 us (97%)
  local copies, waits for them, and re-layouts  2.31 us (2%)
    pallas_call x1, Pallas kernels, shards(): pl.pallas_call(kernel, out_shape=jax.ShapeDtypeStruct((32, LAGS, 8 * LANE...  115 us

profile of v4, /device:TPU:1, one launch (start us, length us, event | category | flops | bytes accessed | tf_op | source)
XLA Modules:
  0.0 117.8 jit_solution(12805059158797202169)
XLA Ops:
  0.0 115.4 %shard_map.17 = f32[32,8,1024]{2,1,0:T(8,128)} custom-call(f32[768,512]{1,0:T(8,128)} %s_ref.1), custom_call_target="tpu_custom_call" | custom-call | flops 38654705664 | bytes 4194304 | tf_op jit(solution)/shard_map/pallas_call | solution.py:512
  115.5 2.3 %copy.3 = f32[32,8,1024]{2,1,0:T(8,128)} copy(f32[32,8,1024]{2,1,0:T(8,128)} %shard_map.17) | data formatting | bytes 2097152

commit v5 on v4

--- a/solution.py
+++ b/solution.py
@@ -52,13 +52,13 @@
     for peer in peers:
         pl.semaphore_signal(barrier, inc=1, device_id=peer, device_id_type=MESH)
 
-    loads = []
-    for q in (1, 3, 2, 0):
-        lanes = pl.ds(pl.multiple_of(lax.rem(x + q, 4) * LANES, LANES), LANES)
-        loads.append(pltpu.make_async_copy(s_ref.at[:, lanes], blocks.at[0, q], load_sem.at[q]))
-        loads[-1].start()
-    for load in loads:
-        load.wait()
+    def channels_of(q):
+        return pl.ds(pl.multiple_of(lax.rem(x + q, 4) * LANES, LANES), LANES)
+
+    loads = {}
+    for q in (0, 1, 3, 2):
+        loads[q] = pltpu.make_async_copy(s_ref.at[:, channels_of(q)], blocks.at[0, q], load_sem.at[q])
+        loads[q].start()
     pl.semaphore_wait(barrier, len(peers))
 
     sent = []
@@ -86,15 +86,25 @@
     fans = []
     for d in range(1, 4):
         fans.append(
-            send(blocks.at[0, d, pl.ds(0, LAGS)], heads.at[x], fan_send.at[4 - d], fan_recv.at[4 - d], along_x(d))
-        )
-    fan_mine = pltpu.make_async_copy(blocks.at[0, 0, pl.ds(0, LAGS)], heads.at[x], fan_own.at[0])
+            send(s_ref.at[pl.ds(0, LAGS), channels_of(d)], heads.at[x], fan_send.at[4 - d], fan_recv.at[4 - d], along_x(d))
+        )
+    fan_mine = pltpu.make_async_copy(s_ref.at[pl.ds(0, LAGS), channels_of(0)], heads.at[x], fan_own.at[0])
     fan_mine.start()
 
     left_0, right_0 = [], []
     for h in range(2):
-        left_0.append(ring(h, 1, 0, 1, parts[h]))
-        right_0.append(ring(2 + h, -1, 0, 3, parts[h]))
+        for n, way, q, to in ((h, 1, 1, left_0), (2 + h, -1, 3, right_0)):
+            to.append(
+                send(
+                    s_ref.at[parts[h], channels_of(q)],
+                    blocks.at[-way % 4, 0, parts[h]],
+                    ring_send.at[n],
+                    ring_recv.at[n],
+                    along_x(way % 4),
+                )
+            )
+    for q in range(4):
+        loads[q].wait()
 
     z_copies, core_copies, own_copies = {}, {}, {}
     tail = pl.ds(LEN, LAGS)
@@ -112,7 +122,7 @@
             device_id_type=MESH,
         )
         sent.append(z_copies[n])
-        if d == 2:
+        if d in (1, 2):
             pl.when(jnp.logical_not(later))(z_copies[n].start)
         else:
             z_copies[n].start()
@@ -126,8 +136,8 @@
         z_copies[n].wait_recv()
         core_copies[6 + n].start()
 
-    def late(do):
-        for n in (2, 4):
+    def late(do, which=(2, 4)):
+        for n in which:
             do(n)
 
     for n in range(6):
@@ -143,11 +153,11 @@
         )
         sent.append(core_copies[6 + n])
 
+    cross(0, 0, whole)
     fan_mine.wait()
     for copy in fans:
         copy.wait_recv()
     over_z = send(heads, heads_z, head_send.at[0], head_recv.at[0], other_half)
-    cross(0, 0, whole)
 
     def seconds(first, q, d):
         cols = slice(q * LANES, (q + 1) * LANES)
@@ -195,13 +205,15 @@
     for h in range(2):
         from_far[h].wait_recv()
         cross(2, 2 + 2 * h, parts[h])
+    pl.when(later)(lambda: late(lambda n: z_copies[n].start(), (1,)))
     rest = [ring(12, 1, 0, 3), ring(13, -1, 0, 1), ring(14, -1, 1, 1), ring(15, 1, 0, 0), ring(16, -1, 0, 2), ring(17, 1, 3, 0)]
     for h in range(2):
         far_1[h].wait_recv()
     seconds(0, 0, 2)
     seconds(0, 1, 2)
-    for n in (3, 1, 5):
+    for n in (3, 5):
         pass_on(n)
+    pl.when(jnp.logical_not(later_z))(lambda: pass_on(1))
 
     def arrived(bb):
         @pl.when(bb == b)
@@ -329,12 +341,12 @@
             add_far(chunk, False)
 
     def before(s):
-        if s == 1:
+        if s == 0:
             pl.when(later)(lambda: late(lambda n: z_copies[n].start()))
         if s == 2:
             pl.when(jnp.logical_not(later_z))(lambda: late(pass_on))
         if s == 4:
-            pl.when(later_z)(lambda: late(pass_on))
+            pl.when(later_z)(lambda: late(pass_on, (1, 2, 4)))
         if s == 8:
             pl.semaphore_signal(ready, inc=1, device_id=other_half, device_id_type=MESH)
             for copy in rest:
@@ -362,7 +374,7 @@
         odd = lax.rem(j, 2)
         e = jnp.where(j < 2, 2, jnp.where(j < 6, 1 + 2 * odd, 0))
         bb = lax.rem(y + e, 4)
-        for i in (1, 2, 4, 8):
+        for i in (0, 2, 4, 8):
             pl.when(s == i)(lambda i=i: before(i))
         fresh = jnp.logical_or(jnp.logical_or(s == 0, s == 2), jnp.logical_or(s == 6, s == jnp.where(far_here, 3, 4)))
 

time: 118 us -> 117 us (level)
  no operation moved by 1% of the time
where the time goes in v5:
time: 117 us
  Pallas kernels  115 us (98%)
  local copies, waits for them, and re-layouts  2.31 us (2%)
    pallas_call x1, Pallas kernels, shards(): pl.pallas_call(kernel, out_shape=jax.ShapeDtypeStruct((32, LAGS, 8 * LANE...  115 us

profile of v5, /device:TPU:1, one launch (start us, length us, event | category | flops | bytes accessed | tf_op | source)
XLA Modules:
  0.0 117.2 jit_solution(5349973699772313053)
XLA Ops:
  0.0 114.8 %shard_map.17 = f32[32,8,1024]{2,1,0:T(8,128)} custom-call(f32[768,512]{1,0:T(8,128)} %s_ref.1), custom_call_target="tpu_custom_call" | custom-call | flops 38654705664 | bytes 4194304 | tf_op jit(solution)/shard_map/pallas_call | solution.py:524
  114.9 2.3 %copy.3 = f32[32,8,1024]{2,1,0:T(8,128)} copy(f32[32,8,1024]{2,1,0:T(8,128)} %shard_map.17) | data formatting | bytes 2097152

commit v6 on v5

--- a/solution.py
+++ b/solution.py
@@ -496,17 +496,7 @@
                             got += last_in[chunk, f, u, cc, 1, w, i]
                         out_ref[:, k, to] = got * scale[k]
 
-    lax.fori_loop(0, 16, step, 0)
-    write(0, 0)
-    write(0, 1)
-    finish(1, 0)
-    finish(1, 1, (1, 0))
-    write(1, 0)
-    write(1, 1, (1, 0))
-    for copy in sent:
-        copy.wait_send()
-
-    for chunk in range(2):
+    def drain(chunk):
         for n in range(2):
             for e in range(4):
                 if e in ends or not whole_sums(chunk, 1, n):
@@ -517,6 +507,18 @@
                     far(chunk, f, way, u).wait_send()
                     for w in range(2):
                         near(chunk, f, way, u, w).wait_send()
+
+    lax.fori_loop(0, 16, step, 0)
+    write(0, 0)
+    write(0, 1)
+    for copy in sent:
+        copy.wait_send()
+    drain(0)
+    finish(1, 0)
+    finish(1, 1, (1, 0))
+    drain(1)
+    write(1, 0)
+    write(1, 1, (1, 0))
 
 
 def shards(strain):

time: 117 us -> 117 us (level)
  no operation moved by 1% of the time
where the time goes in v6:
time: 117 us
  Pallas kernels  115 us (98%)
  local copies, waits for them, and re-layouts  2.31 us (2%)
    pallas_call x1, Pallas kernels, shards(): pl.pallas_call(kernel, out_shape=jax.ShapeDtypeStruct((32, LAGS, 8 * LANE...  115 us

profile of v6, /device:TPU:1, one launch (start us, length us, event | category | flops | bytes accessed | tf_op | source)
XLA Modules:
  0.0 117.0 jit_solution(7389543544875845954)
XLA Ops:
  0.0 114.7 %shard_map.17 = f32[32,8,1024]{2,1,0:T(8,128)} custom-call(f32[768,512]{1,0:T(8,128)} %s_ref.1), custom_call_target="tpu_custom_call" | custom-call | flops 38654705664 | bytes 4194304 | tf_op jit(solution)/shard_map/pallas_call | solution.py:526
  114.7 2.3 %copy.3 = f32[32,8,1024]{2,1,0:T(8,128)} copy(f32[32,8,1024]{2,1,0:T(8,128)} %shard_map.17) | data formatting | bytes 2097152
